TPU v7x, 32 devices: a whole 2x2x4 slice. The times are simulated.
32 devices in a mesh: section: 4 (over y, x), nodes: 8 (over z, core).
Axes of the slice: x: 2, y: 2, z: 4, core: 2. Of those that a mesh axis runs over, the one named last changes fastest.
Arguments:
- features: float32 [4, 2048, 256], P(None, 'nodes'), may hold values from -18 to 18
- cotangent: float32 [4, 2048, 256], P(None, 'nodes'), may hold values from -6 to 6
- train_mask: int32 [4, 2048], P(None, 'nodes'), may hold values 0 or 1
- degree: int32 [4, 2048], P(None, 'nodes'), may hold values from 2 to 8, as said below
- neighbours: int32 [4, 2048, 8], P(None, 'nodes'), may hold values from 0 to 287, as said below
- send_rows: int32 [4, 256], P(None, 'nodes'), may hold values from 0 to 255, as said below
- w_left: float32 [2, 256, 256], replicated, may hold values from -0.375 to 0.375
- w_right: float32 [2, 256, 256], replicated, may hold values from -0.375 to 0.375
- w_res: float32 [2, 256, 256], replicated, may hold values from -0.1875 to 0.1875
- attn_vec: float32 [2, 256], replicated, may hold values from -1.5 to 1.5
- bn_gain: float32 [2, 256], replicated, may hold values from 0.5 to 1.5
- bn_shift: float32 [2, 256], replicated, may hold values from -2 to 2
Outputs:
- outputs: float32 [4, 2048, 256], P('section', 'nodes')
- input_grad: float32 [4, 2048, 256], P('section', 'nodes')
- grad_left: float32 [2, 256, 256], replicated
- grad_right: float32 [2, 256, 256], replicated
- grad_res: float32 [2, 256, 256], replicated
- grad_vec: float32 [2, 256], replicated
- grad_gain: float32 [2, 256], replicated
- grad_shift: float32 [2, 256], replicated
Inputs may be any that keep to these rules, and one draw needn't show every extreme that they name: `degree`: each node has between 2 and 8 live slots; on every partition some node uses all 8. `neighbours`: an entry below 256 is a row of the same partition in that micro-batch, and slot 0 is the node itself; an entry 256 + q * 4 + s is the s-th row that partition q sends to this partition in that micro-batch. `send_rows`: partition q's entries p * 4 to p * 4 + 3 name the local rows that q sends to partition p in that micro-batch.
All inputs are finite; a program needn't handle non-finite values. No bound on the sum of `train_mask` on one device may be relied on, other than what follows from the above.
Results may differ from a plain program's by a relative error of at most 0.0003.
Values sent between devices are 32-bit elements; how exact they have to be, the bound alone decides.
A program may use at most 128 MiB of HBM per device.

v0:
```python
import math

import jax
import jax.numpy as jnp
from jax import lax
from jax.sharding import PartitionSpec as P

HEADS = 4


MASKED_SCORE = -1e30
VARIANCE_EPS = 1e-05
PRECISE = lax.Precision.HIGHEST


def passed_along(block, axis, distance):
    devices = range(lax.axis_size(axis))
    route = [(i - distance, i) for i in devices if i - distance in devices]
    return lax.ppermute(block, axis, route)


def matmul(lhs_rows, rhs_rows):
    return jnp.dot(lhs_rows, rhs_rows, precision=PRECISE, preferred_element_type=jnp.float32)


def attend(row_table, right_rows, slot_index, slot_live, vector):
    node_count, feat_width = right_rows.shape
    slot_count = slot_index.shape[1]
    head_width = feat_width // HEADS
    picked = jnp.take(row_table, slot_index, axis=0)
    activated = jax.nn.silu(picked + right_rows[:, None, :])
    scores = jnp.sum(
        (activated * vector).reshape(node_count, slot_count, HEADS, head_width), axis=3
    )
    scores = jnp.where(slot_live[:, :, None], scores, MASKED_SCORE)
    highest = jnp.max(scores, axis=1, keepdims=True)
    weights = jnp.exp(scores - highest)
    weights = weights / jnp.sum(weights, axis=1, keepdims=True)
    values = picked.reshape(node_count, slot_count, HEADS, head_width)
    joined = jnp.einsum("nkh,nkhc->nhc", weights, values, precision=PRECISE)
    return joined.reshape(node_count, feat_width)


def attend_all(row_table, right_rows, slot_index, slot_live, vector):
    node_count = right_rows.shape[0]
    block_rows = math.gcd(node_count, 512)
    blocks = node_count // block_rows

    def one_block(pieces):
        return attend(row_table, pieces[0], pieces[1], pieces[2], vector)

    result = lax.map(
        one_block,
        (
            right_rows.reshape(blocks, block_rows, -1),
            slot_index.reshape(blocks, block_rows, -1),
            slot_live.reshape(blocks, block_rows, -1),
        ),
    )
    return result.reshape(node_count, -1)


def attend_back(row_table, right_rows, slot_index, slot_live, vector, upstream):
    node_count = right_rows.shape[0]
    block_rows = math.gcd(node_count, 512)
    blocks = node_count // block_rows

    def one_block(carried, pieces):
        table_sum, vector_sum = carried
        block_right, block_index, block_live, block_up = pieces

        def local_part(table_in, right_in, vector_in):
            return attend(table_in, right_in, block_index, block_live, vector_in)

        unused_out, pull_back = jax.vjp(local_part, row_table, block_right, vector)
        grad_table, grad_right, grad_vector = pull_back(block_up)
        return ((table_sum + grad_table, vector_sum + grad_vector), grad_right)

    start = (jnp.zeros_like(row_table), jnp.zeros_like(vector))
    (table_sum, vector_sum), right_grad = lax.scan(
        one_block,
        start,
        (
            right_rows.reshape(blocks, block_rows, -1),
            slot_index.reshape(blocks, block_rows, -1),
            slot_live.reshape(blocks, block_rows, -1),
            upstream.reshape(blocks, block_rows, -1),
        ),
    )
    return (table_sum, right_grad.reshape(node_count, -1), vector_sum)


def take_slot(buffer, batch_index):
    return lax.dynamic_index_in_dim(buffer, batch_index, 0, False)


def store_slot(buffer, new_value, batch_index, active):
    previous = lax.dynamic_index_in_dim(buffer, batch_index, 0, False)
    return lax.dynamic_update_index_in_dim(
        buffer, jnp.where(active, new_value, previous), batch_index, 0
    )


def body(
    features,
    cotangent,
    train_mask,
    degree,
    neighbours,
    send_rows,
    w_left,
    w_right,
    w_res,
    attn_vec,
    bn_gain,
    bn_shift,
):
    section_count = lax.axis_size("section")
    section_index = lax.axis_index("section")
    batch_count, node_rows, feat_width = features.shape
    halo_rows = send_rows.shape[1]
    total_rows = node_rows * lax.axis_size("nodes")
    layer_count = w_left.shape[0]
    layer_index = section_index // 2
    is_post = section_index % 2 == 1
    is_first = section_index == 0
    is_last = section_index == section_count - 1
    left_weight = w_left[layer_index]
    right_weight = w_right[layer_index]
    skip_weight = w_res[layer_index]
    score_vector = attn_vec[layer_index]
    norm_gain = bn_gain[layer_index]
    norm_shift = bn_shift[layer_index]
    live_all = jnp.arange(neighbours.shape[2], dtype=jnp.int32)[None, None, :] < degree[:, :, None]
    tick_count = batch_count + section_count - 1
    plain_rows = jnp.zeros((node_rows, feat_width), jnp.float32)
    plain_pair = jnp.zeros((2, feat_width), jnp.float32)
    plain_square = jnp.zeros((feat_width, feat_width), jnp.float32)
    plain_column = jnp.zeros((feat_width,), jnp.float32)
    plain_halo = jnp.zeros((halo_rows, feat_width), jnp.float32)
    kept_inputs = jnp.zeros((batch_count, node_rows, feat_width), jnp.float32)
    kept_moments = jnp.zeros((batch_count, 2, feat_width), jnp.float32)
    finished = jnp.zeros((batch_count, node_rows, feat_width), jnp.float32)
    arriving = plain_rows
    for tick_index in range(tick_count):
        batch_index = tick_index - section_index
        active = (batch_index >= 0) & (batch_index < batch_count)
        batch_index = jnp.clip(batch_index, 0, batch_count - 1)
        source = jnp.where(is_first, take_slot(features, batch_index), arriving)
        sending = take_slot(send_rows, batch_index)
        slot_index = take_slot(neighbours, batch_index)
        slot_live = take_slot(live_all, batch_index)

        def attend_project(source_rows):
            return (matmul(source_rows, left_weight), matmul(source_rows, right_weight), plain_pair)

        def norm_partial(source_rows):
            sums = jnp.stack(
                [jnp.sum(source_rows, axis=0), jnp.sum(source_rows * source_rows, axis=0)]
            )
            return (plain_rows, plain_rows, sums)

        left_rows, right_rows, partial_value = lax.cond(
            is_post, norm_partial, attend_project, source
        )
        halo_table = lax.all_to_all(
            jnp.take(left_rows, sending, axis=0), "nodes", split_axis=0, concat_axis=0, tiled=True
        )
        moment_sums = lax.psum(partial_value, "nodes")

        def attend_finish(source_rows):
            row_table = jnp.concatenate([left_rows, halo_table], axis=0)
            joined = attend_all(row_table, right_rows, slot_index, slot_live, score_vector)
            return (joined + matmul(source_rows, skip_weight), plain_pair)

        def norm_finish(source_rows):
            mean_row = moment_sums[0] / total_rows
            inverse = lax.rsqrt(moment_sums[1] / total_rows - mean_row * mean_row + VARIANCE_EPS)
            scaled = norm_gain * ((source_rows - mean_row) * inverse) + norm_shift
            return (jax.nn.elu(scaled), jnp.stack([mean_row, inverse]))

        leaving, moments = lax.cond(is_post, norm_finish, attend_finish, source)
        kept_inputs = store_slot(kept_inputs, source, batch_index, active)
        kept_moments = store_slot(kept_moments, moments, batch_index, active)
        finished = store_slot(finished, leaving, batch_index, active)
        arriving = passed_along(leaving, "section", 1)
    total_left = plain_square
    total_right = plain_square
    total_skip = plain_square
    total_vector = plain_column
    total_gain = plain_column
    total_shift = plain_column
    input_grads = jnp.zeros((batch_count, node_rows, feat_width), jnp.float32)
    returning = plain_rows
    for tick_index in range(tick_count):
        batch_index = tick_index - (section_count - 1 - section_index)
        active = (batch_index >= 0) & (batch_index < batch_count)
        batch_index = jnp.clip(batch_index, 0, batch_count - 1)
        masked_grad = (
            take_slot(cotangent, batch_index)
            * take_slot(train_mask, batch_index).astype(jnp.float32)[:, None]
        )
        upstream = jnp.where(is_last, masked_grad, returning)
        source = take_slot(kept_inputs, batch_index)
        moments = take_slot(kept_moments, batch_index)
        sending = take_slot(send_rows, batch_index)
        slot_index = take_slot(neighbours, batch_index)
        slot_live = take_slot(live_all, batch_index)

        def attend_project(source_rows):
            return (
                matmul(source_rows, left_weight),
                matmul(source_rows, right_weight),
                plain_pair,
                plain_rows,
                plain_rows,
                plain_rows,
            )

        def norm_partial(source_rows):
            normed = (source_rows - moments[0]) * moments[1]
            scaled = norm_gain * normed + norm_shift
            scaled_grad = upstream * jnp.where(scaled > 0, 1.0, jnp.exp(jnp.minimum(scaled, 0.0)))
            normed_grad = scaled_grad * norm_gain
            sums = jnp.stack([jnp.sum(normed_grad, axis=0), jnp.sum(normed_grad * normed, axis=0)])
            return (plain_rows, plain_rows, sums, normed, normed_grad, scaled_grad)

        left_rows, right_rows, partial_value, normed, normed_grad, scaled_grad = lax.cond(
            is_post, norm_partial, attend_project, source
        )
        halo_table = lax.all_to_all(
            jnp.take(left_rows, sending, axis=0), "nodes", split_axis=0, concat_axis=0, tiled=True
        )
        grad_sums = lax.psum(partial_value, "nodes")

        def attend_middle(source_rows):
            row_table = jnp.concatenate([left_rows, halo_table], axis=0)
            table_grad, right_grad, vector_grad = attend_back(
                row_table, right_rows, slot_index, slot_live, score_vector, upstream
            )
            return (table_grad[:node_rows], right_grad, table_grad[node_rows:], vector_grad)

        def norm_middle(source_rows):
            mixed_grad = moments[1] * (
                normed_grad - grad_sums[0] / total_rows - normed * (grad_sums[1] / total_rows)
            )
            return (mixed_grad, plain_rows, plain_halo, plain_column)

        first_grad, right_grad, halo_grad, vector_grad = lax.cond(
            is_post, norm_middle, attend_middle, source
        )
        returned = lax.all_to_all(halo_grad, "nodes", split_axis=0, concat_axis=0, tiled=True)

        def attend_last(source_rows):
            left_grad = first_grad.at[sending].add(returned)
            source_grad = (
                matmul(left_grad, left_weight.T)
                + matmul(right_grad, right_weight.T)
                + matmul(upstream, skip_weight.T)
            )
            return (
                source_grad,
                matmul(source_rows.T, left_grad),
                matmul(source_rows.T, right_grad),
                matmul(source_rows.T, upstream),
                plain_column,
                plain_column,
            )

        def norm_last(source_rows):
            return (
                first_grad,
                plain_square,
                plain_square,
                plain_square,
                jnp.sum(scaled_grad * normed, axis=0),
                jnp.sum(scaled_grad, axis=0),
            )

        source_grad, step_left, step_right, step_skip, step_gain, step_shift = lax.cond(
            is_post, norm_last, attend_last, source
        )
        total_left = total_left + jnp.where(active, step_left, 0.0)
        total_right = total_right + jnp.where(active, step_right, 0.0)
        total_skip = total_skip + jnp.where(active, step_skip, 0.0)
        total_vector = total_vector + jnp.where(active, vector_grad, 0.0)
        total_gain = total_gain + jnp.where(active, step_gain, 0.0)
        total_shift = total_shift + jnp.where(active, step_shift, 0.0)
        input_grads = store_slot(input_grads, source_grad, batch_index, active)
        returning = passed_along(source_grad, "section", -1)
    layer_pick = (jnp.arange(layer_count) == layer_index).astype(jnp.float32)
    summed = lax.psum(
        (
            layer_pick[:, None, None] * total_left,
            layer_pick[:, None, None] * total_right,
            layer_pick[:, None, None] * total_skip,
            layer_pick[:, None] * total_vector,
            layer_pick[:, None] * total_gain,
            layer_pick[:, None] * total_shift,
        ),
        ("section", "nodes"),
    )
    placed_out, placed_grad = (
        lax.psum_scatter(
            jnp.where(is_last, finished, 0.0), "section", scatter_dimension=0, tiled=True
        ),
        lax.psum_scatter(
            jnp.where(is_first, input_grads, 0.0), "section", scatter_dimension=0, tiled=True
        ),
    )
    return (
        placed_out,
        placed_grad,
        summed[0],
        summed[1],
        summed[2],
        summed[3],
        summed[4],
        summed[5],
    )


def solution(mesh):
    return jax.shard_map(
        body,
        mesh=mesh,
        in_specs=(
            P(None, "nodes", None),
            P(None, "nodes", None),
            P(None, "nodes"),
            P(None, "nodes"),
            P(None, "nodes", None),
            P(None, "nodes"),
            P(),
            P(),
            P(),
            P(),
            P(),
            P(),
        ),
        out_specs=(
            P("section", "nodes", None),
            P("section", "nodes", None),
            P(),
            P(),
            P(),
            P(),
            P(),
            P(),
        ),
        check_vma=False,
    )
```

profile of v0, /device:TPU:0, one launch (start us, length us, event | category | flops | bytes accessed | tf_op | source)
XLA Modules:
  0.0 1134.2 jit_solution(7559215210112000487)
XLA Ops:
  20.8 17.2 %psum.140 = f32[2,256]{1,0:T(2,128)S(1)} all-reduce(f32[2,256]{1,0:T(2,128)S(1)} %get-tuple-element.2196), channel_id=1, replica_groups=mesh['section'=4,'nodes'=8] {'nodes'}, use_global_device_ids=true, to_apply=%region_4.6 | all-reduce | flops 512 | bytes 4096 | tf_op jit(solution)/shard_map/psum | solution.py:169
  43.3 17.0 %conditional.36 = (f32[256,256]{1,0:T(8,128)S(1)}, f32[2,256]{1,0:T(2,128)S(1)}) conditional(s32[]{:T(128)} %convert_element_type.160, (pred[4,256,8]{1,2,0:T(8,128)(4,1)S(1)}, s32[]{:T(128)}, f32[8,4,256]{2,1,0:T(4,128)S(1)}, f32[256,256]{1,0:T(8,128)S(1)}, s32[4,256,8]{1,2,0:T(8,128)S(1)}, /*index=5*/f32[256,256]{1,0:T(8,128)S(1)}, ...), branch_computations={%region_5.11_spmd, %region_9.12_spmd} | conditional | flops 206712832 | bytes 18318364 | solution.py:182
  72.6 17.1 %psum.141 = f32[2,256]{1,0:T(2,128)S(1)} all-reduce(f32[2,256]{1,0:T(2,128)S(1)} %get-tuple-element.2200), channel_id=1, replica_groups=mesh['section'=4,'nodes'=8] {'nodes'}, use_global_device_ids=true, to_apply=%region_14.17 | all-reduce | flops 512 | bytes 4096 | tf_op jit(solution)/shard_map/psum | solution.py:169
  89.7 17.0 %conditional.38 = (f32[256,256]{1,0:T(8,128)S(1)}, f32[2,256]{1,0:T(2,128)S(1)}) conditional(s32[]{:T(128)} %convert_element_type.160, (pred[4,256,8]{1,2,0:T(8,128)(4,1)S(1)}, s32[]{:T(128)}, f32[8,4,256]{2,1,0:T(4,128)S(1)}, f32[256,256]{1,0:T(8,128)S(1)}, s32[4,256,8]{1,2,0:T(8,128)S(1)}, /*index=5*/f32[256,256]{1,0:T(8,128)S(1)}, ...), branch_computations={%region_15.21_spmd, %region_19.22_spmd} | conditional | flops 206712832 | bytes 18318364 | solution.py:182
  92.0 8.6 gather_fusion.8
  119.0 17.1 %psum.142 = f32[2,256]{1,0:T(2,128)S(1)} all-reduce(f32[2,256]{1,0:T(2,128)S(1)} %get-tuple-element.2204), channel_id=1, replica_groups=mesh['section'=4,'nodes'=8] {'nodes'}, use_global_device_ids=true, to_apply=%region_24.27 | all-reduce | flops 512 | bytes 4096 | tf_op jit(solution)/shard_map/psum | solution.py:169
  136.0 17.2 %conditional.40 = (f32[256,256]{1,0:T(8,128)S(1)}, f32[2,256]{1,0:T(2,128)S(1)}) conditional(s32[]{:T(128)} %convert_element_type.160, (pred[4,256,8]{1,2,0:T(8,128)(4,1)S(1)}, s32[]{:T(128)}, f32[8,4,256]{2,1,0:T(4,128)S(1)}, f32[256,256]{1,0:T(8,128)S(1)}, s32[4,256,8]{1,2,0:T(8,128)S(1)}, /*index=5*/f32[256,256]{1,0:T(8,128)S(1)}, ...), branch_computations={%region_25.31_spmd, %region_29.32_spmd} | conditional | flops 206712832 | bytes 18318364 | solution.py:182
  138.6 8.6 gather_fusion.9
  165.0 17.1 %psum.143 = f32[2,256]{1,0:T(2,128)S(1)} all-reduce(f32[2,256]{1,0:T(2,128)S(1)} %get-tuple-element.2208), channel_id=1, replica_groups=mesh['section'=4,'nodes'=8] {'nodes'}, use_global_device_ids=true, to_apply=%region_34.37 | all-reduce | flops 512 | bytes 4096 | tf_op jit(solution)/shard_map/psum | solution.py:169
  182.1 17.0 %conditional.42 = (f32[256,256]{1,0:T(8,128)S(1)}, f32[2,256]{1,0:T(2,128)S(1)}) conditional(s32[]{:T(128)} %convert_element_type.160, (pred[4,256,8]{1,2,0:T(8,128)(4,1)S(1)}, s32[]{:T(128)}, f32[8,4,256]{2,1,0:T(4,128)S(1)}, f32[256,256]{1,0:T(8,128)S(1)}, s32[4,256,8]{1,2,0:T(8,128)S(1)}, /*index=5*/f32[256,256]{1,0:T(8,128)S(1)}, ...), branch_computations={%region_35.41_spmd, %region_39.42_spmd} | conditional | flops 206712832 | bytes 18318364 | solution.py:182
  184.3 8.6 gather_fusion.10
  210.8 17.1 %psum.144 = f32[2,256]{1,0:T(2,128)S(1)} all-reduce(f32[2,256]{1,0:T(2,128)S(1)} %get-tuple-element.2212), channel_id=1, replica_groups=mesh['section'=4,'nodes'=8] {'nodes'}, use_global_device_ids=true, to_apply=%region_44.47 | all-reduce | flops 512 | bytes 4096 | tf_op jit(solution)/shard_map/psum | solution.py:169
  227.8 17.0 %conditional.44 = (f32[256,256]{1,0:T(8,128)S(1)}, f32[2,256]{1,0:T(2,128)S(1)}) conditional(s32[]{:T(128)} %convert_element_type.160, (pred[4,256,8]{1,2,0:T(8,128)(4,1)S(1)}, s32[]{:T(128)}, f32[8,4,256]{2,1,0:T(4,128)S(1)}, f32[256,256]{1,0:T(8,128)S(1)}, s32[4,256,8]{1,2,0:T(8,128)S(1)}, /*index=5*/f32[256,256]{1,0:T(8,128)S(1)}, ...), branch_computations={%region_45.51_spmd, %region_49.52_spmd} | conditional | flops 206712832 | bytes 18318364 | solution.py:182
  230.1 8.6 gather_fusion.11
  251.0 12.6 %conditional.45 = (f32[256,256]{1,0:T(8,128)S(1)}, f32[256,256]{1,0:T(8,128)S(1)}, f32[2,256]{1,0:T(2,128)S(1)}) conditional(s32[]{:T(128)} %convert_element_type.160, (f32[256,256]{1,0:T(8,128)S(1)}, f32[256,256]{1,0:T(8,128)S(1)}, f32[256,256]{1,0:T(8,128)S(1)}) %tuple.408, f32[256,256]{1,0:T(8,128)S(1)} %get-tuple-element.3449), branch_computations={%region_50.53_spmd, %region_51.56_spmd} | conditional | flops 402653184 | bytes 1574940 | solution.py:163
  268.3 17.1 %psum.145 = f32[2,256]{1,0:T(2,128)S(1)} all-reduce(f32[2,256]{1,0:T(2,128)S(1)} %get-tuple-element.2216), channel_id=1, replica_groups=mesh['section'=4,'nodes'=8] {'nodes'}, use_global_device_ids=true, to_apply=%region_54.57 | all-reduce | flops 512 | bytes 4096 | tf_op jit(solution)/shard_map/psum | solution.py:169
  285.4 17.0 %conditional.46 = (f32[256,256]{1,0:T(8,128)S(1)}, f32[2,256]{1,0:T(2,128)S(1)}) conditional(s32[]{:T(128)} %convert_element_type.160, (pred[4,256,8]{1,2,0:T(8,128)(4,1)S(1)}, s32[]{:T(128)}, f32[8,4,256]{2,1,0:T(4,128)S(1)}, f32[256,256]{1,0:T(8,128)S(1)}, s32[4,256,8]{1,2,0:T(8,128)S(1)}, /*index=5*/f32[256,256]{1,0:T(8,128)S(1)}, ...), branch_computations={%region_55.61_spmd, %region_59.62_spmd} | conditional | flops 206712832 | bytes 18318364 | solution.py:182
  287.6 8.6 gather_fusion.12
  318.0 17.1 %psum.146 = f32[2,256]{1,0:T(2,128)S(1)} all-reduce(f32[2,256]{1,0:T(2,128)S(1)} %get-tuple-element.2220), channel_id=1, replica_groups=mesh['section'=4,'nodes'=8] {'nodes'}, use_global_device_ids=true, to_apply=%region_64.67 | all-reduce | flops 512 | bytes 4096 | tf_op jit(solution)/shard_map/psum | solution.py:169
  335.0 15.3 %conditional.48 = (f32[256,256]{1,0:T(8,128)S(1)}, f32[2,256]{1,0:T(2,128)S(1)}) conditional(s32[]{:T(128)} %convert_element_type.160, (pred[4,256,8]{1,2,0:T(8,128)(4,1)S(1)}, s32[]{:T(128)}, f32[8,4,256]{2,1,0:T(4,128)S(1)}, f32[256,256]{1,0:T(8,128)S(1)}, s32[4,256,8]{1,2,0:T(8,128)S(1)}, /*index=5*/f32[256,256]{1,0:T(8,128)S(1)}, ...), branch_computations={%region_65.71_spmd, %region_69.72_spmd} | conditional | flops 206712832 | bytes 18318364 | solution.py:182
  335.6 8.6 gather_fusion.13
  357.1 17.6 %psum.147 = f32[2,256]{1,0:T(2,128)} all-reduce(f32[2,256]{1,0:T(2,128)S(1)} %get-tuple-element.2231), channel_id=1, replica_groups=mesh['section'=4,'nodes'=8] {'nodes'}, use_global_device_ids=true, to_apply=%region_75.78 | all-reduce | flops 512 | bytes 4096 | tf_op jit(solution)/shard_map/psum | solution.py:234
  374.7 36.1 %conditional.50 = (f32[256,256]{1,0:T(8,128)S(1)}, f32[256,256]{0,1:T(8,128)}, f32[32,256]{1,0:T(8,128)S(1)}, f32[256]{0:T(256)S(1)}) conditional(s32[]{:T(128)} %convert_element_type.160, (f32[8,4,256]{2,1,0:T(4,128)S(1)}, f32[256,256]{1,0:T(8,128)S(1)}, s32[4,256,8]{1,2,0:T(8,128)S(1)}, s32[]{:T(128)}, pred[4,256,8]{1,2,0:T(8,128)(4,1)S(1)}, ...), branch_computations={%region_76.89_spmd, %region_86.90_spmd} | conditional | flops 15922944 | bytes 36079256 | solution.py:249
  376.7 8.6 gather_fusion
  396.5 12.4 %scatter_custom_fusion = f32[288,256]{1,0:T(8,128)} fusion(s32[2048]{0:T(1024)} %reshape.1215, f32[256,8,256]{2,1,0:T(8,128)S(1)} %copy.407, f32[]{:T(128)} %constant.1122.clone), kind=kCustom, calls=%fused_computation.303 | custom fusion | flops 524288 | bytes 2392576 | tf_op jit(solution)/shard_map/cond/branch_0_fun/while/body/eval_jaxpr/transpose(jvp(jit(_take)))/scatter-add | solution.py:30
  447.1 17.6 %psum.148 = f32[2,256]{1,0:T(2,128)} all-reduce(f32[2,256]{1,0:T(2,128)S(1)} %get-tuple-element.2241), channel_id=1, replica_groups=mesh['section'=4,'nodes'=8] {'nodes'}, use_global_device_ids=true, to_apply=%region_96.100 | all-reduce | flops 512 | bytes 4096 | tf_op jit(solution)/shard_map/psum | solution.py:234
  464.8 37.6 %conditional.53 = (f32[256,256]{1,0:T(8,128)S(1)}, f32[256,256]{0,1:T(8,128)}, f32[32,256]{1,0:T(8,128)S(1)}, f32[256]{0:T(256)S(1)}) conditional(s32[]{:T(128)} %convert_element_type.160, (f32[8,4,256]{2,1,0:T(4,128)S(1)}, f32[256,256]{1,0:T(8,128)S(1)}, s32[4,256,8]{1,2,0:T(8,128)S(1)}, s32[]{:T(128)}, pred[4,256,8]{1,2,0:T(8,128)(4,1)S(1)}, ...), branch_computations={%region_97.110_spmd, %region_107.111_spmd} | conditional | flops 15922944 | bytes 36078748 | solution.py:249
  468.1 8.6 gather_fusion.1
  487.9 12.3 %scatter_custom_fusion.8 = f32[288,256]{1,0:T(8,128)} fusion(s32[2048]{0:T(1024)S(1)} %reshape.1279, f32[256,8,256]{2,1,0:T(8,128)S(1)} %copy.410, f32[]{:T(128)} %constant.1136.clone), kind=kCustom, calls=%fused_computation.340 | custom fusion | flops 524288 | bytes 2392068 | tf_op jit(solution)/shard_map/cond/branch_0_fun/while/body/eval_jaxpr/transpose(jvp(jit(_take)))/scatter-add | solution.py:30
  538.7 17.1 %psum.149 = f32[2,256]{1,0:T(2,128)S(1)} all-reduce(f32[2,256]{1,0:T(2,128)S(1)} %get-tuple-element.2251), channel_id=1, replica_groups=mesh['section'=4,'nodes'=8] {'nodes'}, use_global_device_ids=true, to_apply=%region_117.121 | all-reduce | flops 512 | bytes 4096 | tf_op jit(solution)/shard_map/psum | solution.py:234
  555.7 37.3 %conditional.56 = (f32[256,256]{1,0:T(8,128)S(1)}, f32[256,256]{0,1:T(8,128)}, f32[32,256]{1,0:T(8,128)S(1)}, f32[256]{0:T(256)S(1)}) conditional(s32[]{:T(128)} %convert_element_type.160, (f32[8,4,256]{2,1,0:T(4,128)S(1)}, f32[256,256]{1,0:T(8,128)S(1)}, s32[4,256,8]{1,2,0:T(8,128)S(1)}, s32[]{:T(128)}, pred[4,256,8]{1,2,0:T(8,128)(4,1)S(1)}, ...), branch_computations={%region_118.131_spmd, %region_128.132_spmd} | conditional | flops 15922944 | bytes 36078748 | solution.py:249
  559.0 8.6 gather_fusion.2
  578.8 12.3 %scatter_custom_fusion.9 = f32[288,256]{1,0:T(8,128)} fusion(s32[2048]{0:T(1024)S(1)} %reshape.1287, f32[256,8,256]{2,1,0:T(8,128)S(1)} %copy.413, f32[]{:T(128)} %constant.1150.clone), kind=kCustom, calls=%fused_computation.377 | custom fusion | flops 524288 | bytes 2392068 | tf_op jit(solution)/shard_map/cond/branch_0_fun/while/body/eval_jaxpr/transpose(jvp(jit(_take)))/scatter-add | solution.py:30
  629.3 17.1 %psum.150 = f32[2,256]{1,0:T(2,128)S(1)} all-reduce(f32[2,256]{1,0:T(2,128)S(1)} %get-tuple-element.2261), channel_id=1, replica_groups=mesh['section'=4,'nodes'=8] {'nodes'}, use_global_device_ids=true, to_apply=%region_138.142 | all-reduce | flops 512 | bytes 4096 | tf_op jit(solution)/shard_map/psum | solution.py:234
  646.3 37.4 %conditional.59 = (f32[256,256]{1,0:T(8,128)S(1)}, f32[256,256]{0,1:T(8,128)}, f32[32,256]{1,0:T(8,128)S(1)}, f32[256]{0:T(256)S(1)}) conditional(s32[]{:T(128)} %convert_element_type.160, (f32[8,4,256]{2,1,0:T(4,128)S(1)}, f32[256,256]{1,0:T(8,128)S(1)}, s32[4,256,8]{1,2,0:T(8,128)S(1)}, s32[]{:T(128)}, pred[4,256,8]{1,2,0:T(8,128)(4,1)S(1)}, ...), branch_computations={%region_139.152_spmd, %region_149.153_spmd} | conditional | flops 15922944 | bytes 36078748 | solution.py:249
  649.7 8.6 gather_fusion.3
  669.5 12.3 %scatter_custom_fusion.10 = f32[288,256]{1,0:T(8,128)} fusion(s32[2048]{0:T(1024)S(1)} %reshape.1295, f32[256,8,256]{2,1,0:T(8,128)S(1)} %copy.416, f32[]{:T(128)} %constant.1164.clone), kind=kCustom, calls=%fused_computation.414 | custom fusion | flops 524288 | bytes 2392068 | tf_op jit(solution)/shard_map/cond/branch_0_fun/while/body/eval_jaxpr/transpose(jvp(jit(_take)))/scatter-add | solution.py:30
  719.8 17.1 %psum.151 = f32[2,256]{1,0:T(2,128)S(1)} all-reduce(f32[2,256]{1,0:T(2,128)S(1)} %get-tuple-element.2271), channel_id=1, replica_groups=mesh['section'=4,'nodes'=8] {'nodes'}, use_global_device_ids=true, to_apply=%region_159.163 | all-reduce | flops 512 | bytes 4096 | tf_op jit(solution)/shard_map/psum | solution.py:234
  736.9 35.9 %conditional.62 = (f32[256,256]{1,0:T(8,128)S(1)}, f32[256,256]{0,1:T(8,128)}, f32[32,256]{1,0:T(8,128)S(1)}, f32[256]{0:T(256)S(1)}) conditional(s32[]{:T(128)} %convert_element_type.160, (f32[8,4,256]{2,1,0:T(4,128)S(1)}, f32[256,256]{1,0:T(8,128)S(1)}, s32[4,256,8]{1,2,0:T(8,128)S(1)}, s32[]{:T(128)}, pred[4,256,8]{1,2,0:T(8,128)(4,1)S(1)}, ...), branch_computations={%region_160.173_spmd, %region_170.174_spmd} | conditional | flops 15922944 | bytes 36078748 | solution.py:249
  758.6 12.3 %scatter_custom_fusion.11 = f32[288,256]{1,0:T(8,128)} fusion(s32[2048]{0:T(1024)S(1)} %reshape.1303, f32[256,8,256]{2,1,0:T(8,128)S(1)} %copy.419, f32[]{:T(128)} %constant.1178.clone), kind=kCustom, calls=%fused_computation.451 | custom fusion | flops 524288 | bytes 2392068 | tf_op jit(solution)/shard_map/cond/branch_0_fun/while/body/eval_jaxpr/transpose(jvp(jit(_take)))/scatter-add | solution.py:30
  807.8 17.1 %psum.152 = f32[2,256]{1,0:T(2,128)S(1)} all-reduce(f32[2,256]{1,0:T(2,128)S(1)} %get-tuple-element.2281), channel_id=1, replica_groups=mesh['section'=4,'nodes'=8] {'nodes'}, use_global_device_ids=true, to_apply=%region_180.184 | all-reduce | flops 512 | bytes 4096 | tf_op jit(solution)/shard_map/psum | solution.py:234
  824.9 35.7 %conditional.65 = (f32[256,256]{1,0:T(8,128)S(1)}, f32[256,256]{0,1:T(8,128)}, f32[32,256]{1,0:T(8,128)S(1)}, f32[256]{0:T(256)S(1)}) conditional(s32[]{:T(128)} %convert_element_type.160, (f32[8,4,256]{2,1,0:T(4,128)S(1)}, f32[256,256]{1,0:T(8,128)S(1)}, s32[4,256,8]{1,2,0:T(8,128)S(1)}, s32[]{:T(128)}, pred[4,256,8]{1,2,0:T(8,128)(4,1)S(1)}, ...), branch_computations={%region_181.194_spmd, %region_191.195_spmd} | conditional | flops 15922944 | bytes 36078748 | solution.py:249
  846.3 12.3 %scatter_custom_fusion.12 = f32[288,256]{1,0:T(8,128)} fusion(s32[2048]{0:T(1024)S(1)} %reshape.1311, f32[256,8,256]{2,1,0:T(8,128)S(1)} %copy.422, f32[]{:T(128)} %constant.1192.clone), kind=kCustom, calls=%fused_computation.488 | custom fusion | flops 524288 | bytes 2392068 | tf_op jit(solution)/shard_map/cond/branch_0_fun/while/body/eval_jaxpr/transpose(jvp(jit(_take)))/scatter-add | solution.py:30
  895.5 17.1 %psum.153 = f32[2,256]{1,0:T(2,128)S(1)} all-reduce(f32[2,256]{1,0:T(2,128)S(1)} %get-tuple-element.2291), channel_id=1, replica_groups=mesh['section'=4,'nodes'=8] {'nodes'}, use_global_device_ids=true, to_apply=%region_201.205 | all-reduce | flops 512 | bytes 4096 | tf_op jit(solution)/shard_map/psum | solution.py:234
  912.6 35.8 %conditional.68 = (f32[256,256]{1,0:T(8,128)S(1)}, f32[256,256]{0,1:T(8,128)}, f32[32,256]{1,0:T(8,128)S(1)}, f32[256]{0:T(256)S(1)}) conditional(s32[]{:T(128)} %convert_element_type.160, (f32[8,4,256]{2,1,0:T(4,128)S(1)}, f32[256,256]{1,0:T(8,128)S(1)}, s32[4,256,8]{1,2,0:T(8,128)S(1)}, s32[]{:T(128)}, pred[4,256,8]{1,2,0:T(8,128)(4,1)S(1)}, ...), branch_computations={%region_202.215_spmd, %region_212.216_spmd} | conditional | flops 15922944 | bytes 36078748 | solution.py:249
  934.1 12.3 %scatter_custom_fusion.13 = f32[288,256]{1,0:T(8,128)} fusion(s32[2048]{0:T(1024)S(1)} %reshape.1319, f32[256,8,256]{2,1,0:T(8,128)S(1)} %copy.425, f32[]{:T(128)} %constant.1206.clone), kind=kCustom, calls=%fused_computation.525 | custom fusion | flops 524288 | bytes 2392068 | tf_op jit(solution)/shard_map/cond/branch_0_fun/while/body/eval_jaxpr/transpose(jvp(jit(_take)))/scatter-add | solution.py:30
  975.2 58.3 %all-reduce.2 = (f32[2,256]{1,0:T(2,128)}, f32[2,256]{1,0:T(2,128)}, f32[2,256]{1,0:T(2,128)}) all-reduce(f32[2,256]{1,0:T(2,128)S(1)} %get-tuple-element.3586, f32[2,256]{1,0:T(2,128)S(1)} %get-tuple-element.3585, f32[2,256]{1,0:T(2,128)S(1)} %get-tuple-element.3584), channel_id=1, replica_groups=mesh['section'=4,'nodes'=8] {'section','nodes'}, use_global_device_ids=true, to_apply=%region_222.226 | all-reduce | flops 1536 | bytes 12288 | tf_op jit(solution)/shard_map/psum | solution.py:292
  1033.5 88.0 %all-reduce.6.cloned.1.call-done = (f32[2,256,256]{2,1,0:T(8,128)}, f32[2,256,256]{2,1,0:T(8,128)}, f32[2,256,256]{2,1,0:T(8,128)}) async-done(((f32[2,256,256]{2,1,0:T(8,128)}, f32[2,256,256]{2,1,0:T(8,128)}, f32[2,256,256]{2,1,0:T(8,128)}), (f32[2,256,256]{2,1,0:T(8,128)}, f32[2,256,256]{2,1,0:T(8,128)}, f32[2,256,256]{2,1,0:T(8,128)})) %all-reduce.6.cloned.1.call-update) | async-done | bytes 1572880 | tf_op jit(solution)/shard_map/psum | solution.py:292
  (1088 shorter events, 607.5 us)
Async XLA Ops:
  10.0 31.0 %copy-start.177 = (s32[32]{0:T(128)}, s32[32]{0:T(128)S(1)}, u32[]{:S(2)}) copy-start(s32[32]{0:T(128)S(1)} %get-tuple-element.3561) | copy-start | bytes 388
  10.1 31.5 %copy-start.176 = (s32[32]{0:T(128)}, s32[32]{0:T(128)S(1)}, u32[]{:S(2)}) copy-start(s32[32]{0:T(128)S(1)} %get-tuple-element.3559) | copy-start | bytes 388
  10.1 32.1 %copy-start.175 = (s32[32]{0:T(128)}, s32[32]{0:T(128)S(1)}, u32[]{:S(2)}) copy-start(s32[32]{0:T(128)S(1)} %get-tuple-element.3583) | copy-start | bytes 388
  10.1 32.6 %copy-start.174 = (s32[32]{0:T(128)}, s32[32]{0:T(128)S(1)}, u32[]{:S(2)}) copy-start(s32[32]{0:T(128)S(1)} %get-tuple-element.3433) | copy-start | bytes 388
  12.3 30.9 %copy-start.188 = (f32[2,256]{1,0:T(2,128)S(1)}, f32[2,256]{1,0:T(2,128)}, u32[]{:S(2)}) copy-start(f32[2,256]{1,0:T(2,128)} %param.99) | copy-start | bytes 6148
  12.3 30.9 %copy-start.50 = (s32[4,256,8]{1,2,0:T(8,128)S(1)}, s32[4,256,8]{1,2,0:T(8,128)}, u32[]{:S(2)}) copy-start(s32[4,256,8]{1,2,0:T(8,128)} %param.92) | copy-start | bytes 98308
  14.5 28.8 %all-to-all-start = ((f32[8,4,256]{2,1,0:T(4,128)}), f32[8,4,256]{2,1,0:T(4,128)S(1)}, u32[]{:S(2)}, u32[]{:S(2)}) async-start(f32[8,4,256]{2,1,0:T(4,128)} %all_to_all.168), calls=%async_computation | async-start | bytes 65536 | tf_op jit(solution)/shard_map/all_to_all | solution.py:166
  60.3 5.2 collective-permute-start
  63.3 311.4 %copy-start.22 = (f32[256,256]{1,0:T(8,128)}, f32[256,256]{1,0:T(8,128)S(1)}, u32[]{:S(2)}) copy-start(f32[256,256]{1,0:T(8,128)S(1)} %fusion.104) | copy-start | bytes 786436
  68.7 21.0 %all-to-all-start.1 = ((f32[8,4,256]{2,1,0:T(4,128)}), f32[8,4,256]{2,1,0:T(4,128)S(1)}, u32[]{:S(2)}, u32[]{:S(2)}) async-start(f32[8,4,256]{2,1,0:T(4,128)} %all_to_all.170), calls=%async_computation.1 | async-start | bytes 65536 | tf_op jit(solution)/shard_map/all_to_all | solution.py:166
  106.7 5.2 collective-permute-start.1
  115.0 21.0 %all-to-all-start.2 = ((f32[8,4,256]{2,1,0:T(4,128)}), f32[8,4,256]{2,1,0:T(4,128)S(1)}, u32[]{:S(2)}, u32[]{:S(2)}) async-start(f32[8,4,256]{2,1,0:T(4,128)} %all_to_all.172), calls=%async_computation.2 | async-start | bytes 65536 | tf_op jit(solution)/shard_map/all_to_all | solution.py:166
  153.3 5.2 collective-permute-start.2
  161.6 20.5 %all-to-all-start.3 = ((f32[8,4,256]{2,1,0:T(4,128)}), f32[8,4,256]{2,1,0:T(4,128)S(1)}, u32[]{:S(2)}, u32[]{:S(2)}) async-start(f32[8,4,256]{2,1,0:T(4,128)} %all_to_all.174), calls=%async_computation.3 | async-start | bytes 65536 | tf_op jit(solution)/shard_map/all_to_all | solution.py:166
  199.1 5.2 collective-permute-start.3
  207.4 20.5 %all-to-all-start.4 = ((f32[8,4,256]{2,1,0:T(4,128)}), f32[8,4,256]{2,1,0:T(4,128)S(1)}, u32[]{:S(2)}, u32[]{:S(2)}) async-start(f32[8,4,256]{2,1,0:T(4,128)} %all_to_all.176), calls=%async_computation.4 | async-start | bytes 65536 | tf_op jit(solution)/shard_map/all_to_all | solution.py:166
  244.8 5.2 collective-permute-start.4
  264.9 20.5 %all-to-all-start.5 = ((f32[8,4,256]{2,1,0:T(4,128)}), f32[8,4,256]{2,1,0:T(4,128)S(1)}, u32[]{:S(2)}, u32[]{:S(2)}) async-start(f32[8,4,256]{2,1,0:T(4,128)} %all_to_all.178), calls=%async_computation.5 | async-start | bytes 65536 | tf_op jit(solution)/shard_map/all_to_all | solution.py:166
  302.4 7.9 collective-permute-start.5
  313.4 21.6 %all-to-all-start.6 = ((f32[8,4,256]{2,1,0:T(4,128)}), f32[8,4,256]{2,1,0:T(4,128)S(1)}, u32[]{:S(2)}, u32[]{:S(2)}) async-start(f32[8,4,256]{2,1,0:T(4,128)} %all_to_all.180), calls=%async_computation.6 | async-start | bytes 65536 | tf_op jit(solution)/shard_map/all_to_all | solution.py:166
  318.0 32.4 %copy-start.20 = (f32[256,256]{1,0:T(8,128)}, f32[256,256]{1,0:T(8,128)S(1)}, u32[]{:S(2)}) copy-start(f32[256,256]{1,0:T(8,128)S(1)} %get-tuple-element.3541) | copy-start | bytes 786436
  353.2 21.5 %all-to-all-start.7 = ((f32[8,4,256]{2,1,0:T(4,128)}), f32[8,4,256]{2,1,0:T(4,128)S(1)}, u32[]{:S(2)}, u32[]{:S(2)}) async-start(f32[8,4,256]{2,1,0:T(4,128)} %all_to_all.182), calls=%async_computation.7 | async-start | bytes 65536 | tf_op jit(solution)/shard_map/all_to_all | solution.py:231
  411.5 9.0 all-to-all-start.8
  428.2 10.0 collective-permute-start.6
  430.7 34.1 %copy-start.2 = (f32[4,256,256]{2,1,0:T(8,128)}, f32[4,256,256]{2,1,0:T(8,128)S(1)}, u32[]{:S(2)}) copy-start(f32[4,256,256]{2,1,0:T(8,128)S(1)} %bitcast_dynamic-update-slice_fusion.18) | copy-start | bytes 3145732
  443.0 21.7 %all-to-all-start.9 = ((f32[8,4,256]{2,1,0:T(4,128)}), f32[8,4,256]{2,1,0:T(4,128)S(1)}, u32[]{:S(2)}, u32[]{:S(2)}) async-start(f32[8,4,256]{2,1,0:T(4,128)} %all_to_all.186), calls=%async_computation.9 | async-start | bytes 65536 | tf_op jit(solution)/shard_map/all_to_all | solution.py:231
  503.0 9.0 all-to-all-start.10
  519.8 10.0 collective-permute-start.7
  522.2 33.5 %copy-start.4 = (f32[4,256,256]{2,1,0:T(8,128)}, f32[4,256,256]{2,1,0:T(8,128)S(1)}, u32[]{:S(2)}) copy-start(f32[4,256,256]{2,1,0:T(8,128)S(1)} %bitcast_dynamic-update-slice_fusion.16) | copy-start | bytes 3145732
  534.6 21.1 %all-to-all-start.11 = ((f32[8,4,256]{2,1,0:T(4,128)}), f32[8,4,256]{2,1,0:T(4,128)S(1)}, u32[]{:S(2)}, u32[]{:S(2)}) async-start(f32[8,4,256]{2,1,0:T(4,128)} %all_to_all.190), calls=%async_computation.11 | async-start | bytes 65536 | tf_op jit(solution)/shard_map/all_to_all | solution.py:231
  593.7 9.0 all-to-all-start.12
  610.4 10.0 collective-permute-start.8
  611.9 34.4 %copy-start.6 = (f32[4,256,256]{2,1,0:T(8,128)}, f32[4,256,256]{2,1,0:T(8,128)S(1)}, u32[]{:S(2)}) copy-start(f32[4,256,256]{2,1,0:T(8,128)S(1)} %bitcast_dynamic-update-slice_fusion.14) | copy-start | bytes 3145732
  625.2 21.1 %all-to-all-start.13 = ((f32[8,4,256]{2,1,0:T(4,128)}), f32[8,4,256]{2,1,0:T(4,128)S(1)}, u32[]{:S(2)}, u32[]{:S(2)}) async-start(f32[8,4,256]{2,1,0:T(4,128)} %all_to_all.194), calls=%async_computation.13 | async-start | bytes 65536 | tf_op jit(solution)/shard_map/all_to_all | solution.py:231
  684.4 9.0 all-to-all-start.14
  687.8 345.8 %reduce-scatter.7.cloned.1.call-start = ((), (), s32[]{:S(2)}) async-start(), calls=%async_computation.23 | async-start | bytes 1310720
  701.2 10.0 collective-permute-start.9
  714.7 22.2 %all-to-all-start.15 = ((f32[8,4,256]{2,1,0:T(4,128)}), f32[8,4,256]{2,1,0:T(4,128)S(1)}, u32[]{:S(2)}, u32[]{:S(2)}) async-start(f32[8,4,256]{2,1,0:T(4,128)} %all_to_all.198), calls=%async_computation.15 | async-start | bytes 65536 | tf_op jit(solution)/shard_map/all_to_all | solution.py:231
  773.5 9.0 all-to-all-start.16
  790.2 10.0 collective-permute-start.10
  803.7 21.2 %all-to-all-start.17 = ((f32[8,4,256]{2,1,0:T(4,128)}), f32[8,4,256]{2,1,0:T(4,128)S(1)}, u32[]{:S(2)}, u32[]{:S(2)}) async-start(f32[8,4,256]{2,1,0:T(4,128)} %all_to_all.202), calls=%async_computation.17 | async-start | bytes 65536 | tf_op jit(solution)/shard_map/all_to_all | solution.py:231
  861.2 9.0 all-to-all-start.18
  877.9 10.0 collective-permute-start.11
  891.4 21.2 %all-to-all-start.19 = ((f32[8,4,256]{2,1,0:T(4,128)}), f32[8,4,256]{2,1,0:T(4,128)S(1)}, u32[]{:S(2)}, u32[]{:S(2)}) async-start(f32[8,4,256]{2,1,0:T(4,128)} %all_to_all.206), calls=%async_computation.19 | async-start | bytes 65536 | tf_op jit(solution)/shard_map/all_to_all | solution.py:231
  949.1 9.0 all-to-all-start.20
  952.4 169.2 %all-reduce.6.cloned.1.call-start = ((), (), s32[]{:S(2)}) async-start(), calls=%async_computation.25 | async-start | bytes 3145728 | tf_op jit(solution)/shard_map/psum | solution.py:292
  969.9 151.7 %reduce-scatter.9.cloned.1.call-start = ((), (), s32[]{:S(2)}) async-start(), calls=%async_computation.24 | async-start | bytes 1310720
  974.9 151.3 %copy-start.1 = (f32[2,256,256]{2,1,0:T(8,128)S(1)}, f32[2,256,256]{2,1,0:T(8,128)}, u32[]{:S(2)}) copy-start(f32[2,256,256]{2,1,0:T(8,128)} %param.96) | copy-start | bytes 1572868
  (177 other events, 1577.0 us)
Sparse Core Ops, SparseCore 0:
  703.9 48.4 reduce-scatter.6
  975.1 46.2 reduce-scatter.8
Sparse Core Ops, SparseCore 1:
  970.0 151.5 all-reduce.5
where the time goes:
time: 1150 us; the launch traced here: 1130 us
  blocking collectives  298 us (26%)
  local copies, waits for them, and re-layouts  262 us (23%)
  other arithmetic  213 us (19%)
  waiting for transfers between devices  182 us (16%)
  starting transfers between devices  92.4 us (8%)
  matrix products  49.7 us (4%)
  between operations  18.8 us (2%)
  loops' own time  18.3 us (2%)
    gather x28, local copies, waits for them, and re-layouts, attend(): picked = jnp.take(row_table, slot_index, axis=0)  154 us
    psum x7, blocking collectives, body(): grad_sums = lax.psum(partial_value, 'nodes')  121 us
    psum x7, blocking collectives, body(): moment_sums = lax.psum(partial_value, 'nodes')  120 us
    psum x1, waiting for transfers between devices, body(): lax.psum((layer_pick[:, None, None] * total_left, layer_pick[:, None, Non...  88 us
    scatter-add x7, other arithmetic, attend(): picked = jnp.take(row_table, slot_index, axis=0)  86.3 us
    ppermute x12, waiting for transfers between devices, passed_along(): return lax.ppermute(block, axis, route)  63.1 us
    psum x1, blocking collectives, body(): lax.psum((layer_pick[:, None, None] * total_left, layer_pick[:, None, Non...  58.3 us
    all_to_all x14, starting transfers between devices, body(): lax.all_to_all(jnp.take(left_rows, sending, axis=0), 'nodes', split_axis=...  49.8 us
  transfers between devices with their start and end apart: 36, of which 20 were waited for; matrix products, arithmetic and copies ran while one was open for 16% of the time, Pallas kernels for 0%

commit v1 on v0

v1 whole, which is shorter than its diff:
```python
import functools
import types

import jax
import jax.numpy as jnp
from jax import lax
from jax.experimental import pallas as pl
from jax.experimental.pallas import tpu as pltpu
from jax.sharding import PartitionSpec as P

HEADS = 4
MASKED_SCORE = -1e30
VARIANCE_EPS = 1e-05
F32 = jnp.float32
BF16 = jnp.bfloat16
MESH = pl.DeviceIdType.MESH
LANES = 128
TILE = 8
CHUNK = 16

FEATURES, MIXED, SUMS, BACK_SUMS, BACK_ROWS, INPUT_ROWS, SMALL = range(7)
EXCHANGES = 7
CORE, SECTION, OUTER, OUTER_BACK, SECTION_BACK, CORE_BACK = range(6)
STAGES = 6


def halves(values):
    high = values.astype(BF16)
    return high, (values - high.astype(F32)).astype(BF16)


def mm(lhs, rhs):
    return jnp.dot(lhs, rhs, preferred_element_type=F32)


def mm_nt(lhs, rhs):
    return lax.dot_general(lhs, rhs, (((1,), (1,)), ((), ())), preferred_element_type=F32)


def mm3(lhs, rhs, product=mm):
    return product(lhs[0], rhs[0]) + product(lhs[1], rhs[0]) + product(lhs[0], rhs[1])


def iota(shape, dim):
    return lax.broadcasted_iota(jnp.int32, shape, dim)


def as_ones(condition):
    return jnp.where(condition, 1.0, 0.0).astype(BF16)


def sizes_of(sections, partitions, rows, width, slots, listed):
    z = types.SimpleNamespace()
    z.sections, z.partitions, z.outer = sections, partitions, partitions // 2
    z.rows, z.width, z.slots, z.listed = rows, width, slots, listed
    z.send = listed // partitions
    z.halo = partitions * TILE
    z.halo_pad = -(-z.halo // LANES) * LANES
    z.table = rows + z.halo_pad
    z.picked = rows + z.halo
    z.share = rows // sections
    z.piece = max(TILE, z.share // z.outer)
    z.owners = z.share // z.piece
    return z


def scratch_of(z):
    R, D, K, T = z.rows, z.width, z.slots, z.table
    S, O = z.sections, z.outer
    half = D // 2
    vmem = {
        "features_in": ((R, D), F32),
        "cotangent_in": ((R, D), F32),
        "mask_in": (None, jnp.int32),
        "degree_in": (None, jnp.int32),
        "slots_in": ((K, R), jnp.int32),
        "listed_in": (None, jnp.int32),
        "weights_in": ((3, 2, D, D), F32),
        "vector_in": ((2, D), F32),
        "gain_in": ((2, D), F32),
        "shift_in": ((2, D), F32),
        "weights_hi": ((2, 3, D, D), BF16),
        "weights_lo": ((2, 3, D, D), BF16),
        "prep": ((LANES, R), F32),
        "prep_t": ((R, LANES), F32),
        "listed_row": ((TILE, max(LANES, z.listed)), F32),
        "pick": ((K - 1, R, T), BF16),
        "pick_t": ((z.picked, (K - 1) * R), BF16),
        "list": ((z.halo, R), BF16),
        "list_t": ((R, z.halo_pad), BF16),
        "ones": ((2 * D, D), BF16),
        "h": ((T, D), F32),
        "h_hi": ((T, D), BF16),
        "h_lo": ((T, D), BF16),
        "ht_hi": ((2, D, T), BF16),
        "ht_lo": ((2, D, T), BF16),
        "table_hi": ((T, D), BF16),
        "table_lo": ((T, D), BF16),
        "taken": ((2, K, R, D), F32),
        "sig": ((2, K, R, D), F32),
        "alpha": ((2, K, R, D), F32),
        "joined": ((2, R, D), F32),
        "right": ((2, R, D), F32),
        "skip": ((R, D), F32),
        "mixed": ((R, D), F32),
        "normed": ((2, R, D), F32),
        "slope": ((2, R, D), F32),
        "halo_normed": ((z.halo, D), F32),
        "halo_slope": ((z.halo, D), F32),
        "pair": ((K, R, 2 * D), BF16),
        "score": ((K, R, D), F32),
        "dpre": ((R, D), F32),
        "dmixed": ((R, D), F32),
        "dm_hi": ((R, D), BF16),
        "dm_lo": ((R, D), BF16),
        "dr_hi": ((R, D), BF16),
        "dr_lo": ((R, D), BF16),
        "dl_hi": ((T, D), BF16),
        "dl_lo": ((T, D), BF16),
        "dleft_self": ((R, D), F32),
        "dleft_hi": (((K - 1) * R, D), BF16),
        "dleft_lo": (((K - 1) * R, D), BF16),
        "dh": ((R, D), F32),
        "outgoing": ((EXCHANGES, z.halo, D), F32),
        "incoming": ((EXCHANGES, z.halo, D), F32),
        "small": ((TILE, D), F32),
        "small_in": ((S, TILE, D), F32),
        "vector_out": ((2, D), F32),
        "gain_out": ((2, D), F32),
        "shift_out": ((2, D), F32),
        "out_rows": ((R, D), F32),
        "grad_rows": ((R, D), F32),
        "sums": ((2, 3, 2, R, half), F32),
        "from_core": ((2, 3, R, half), F32),
        "from_section": ((2, S - 1, 3, z.share, half), F32),
        "from_outer": ((2, O, 3, z.piece, half), F32),
        "whole": ((2, 3, R, half), F32),
    }
    return vmem


SEMAPHORES = {
    "load": (12,),
    "give": (EXCHANGES,),
    "take": (EXCHANGES,),
    "give_small": (1,),
    "take_small": (1,),
    "give_stage": (2, 3, STAGES),
    "take_stage": (2, 3, STAGES),
    "give_back": (2, 3),
    "take_back": (2, 3),
    "store": (16,),
}


def kernel(z, names, *refs):
    features, cotangent, train_mask, degree, neighbours, send_rows = refs[:6]
    w_left, w_right, w_res, attn_vec, bn_gain, bn_shift = refs[6:12]
    out, grad_in, g_left, g_right, g_res, g_vec, g_gain, g_shift = refs[12:20]
    v = types.SimpleNamespace(**dict(zip(names, refs[20:])))
    grads_out = (g_left, g_right, g_res)
    R, D, K, T = z.rows, z.width, z.slots, z.table
    S, N, O = z.sections, z.partitions, z.outer
    half = D // 2
    total_rows = R * N
    sec = lax.axis_index("section")
    me = lax.axis_index("nodes")
    core = lax.rem(me, 2)
    outer = lax.div(me, 2)
    mate = me + 1 - 2 * core

    barrier = pltpu.get_barrier_semaphore()

    def greet(step, carry):
        pl.semaphore_signal(
            barrier, inc=1, device_id={"nodes": lax.rem(me + step, N)}, device_id_type=MESH
        )
        return carry

    lax.fori_loop(1, N, greet, 0)
    for step in range(1, S):
        pl.semaphore_signal(
            barrier, inc=1, device_id={"section": lax.rem(sec + step, S)}, device_id_type=MESH
        )

    loads = []
    for source, target in (
        (features.at[sec], v.features_in),
        (send_rows, v.listed_in),
        (w_left, v.weights_in.at[0]),
        (w_right, v.weights_in.at[1]),
        (w_res, v.weights_in.at[2]),
        (neighbours.at[sec], v.slots_in),
        (degree, v.degree_in),
        (train_mask, v.mask_in),
        (attn_vec, v.vector_in),
        (bn_gain, v.gain_in),
        (bn_shift, v.shift_in),
        (cotangent.at[sec], v.cotangent_in),
    ):
        copy = pltpu.make_async_copy(source, target, v.load.at[len(loads)])
        copy.start()
        loads.append(copy)

    def rows_loop(body, start):
        return lax.fori_loop(0, R // CHUNK, body, start)

    def chunk(i):
        return pl.ds(pl.multiple_of(i * CHUNK, CHUNK), CHUNK)

    def fold(values):
        return jnp.sum(values.reshape(values.shape[0] // TILE, TILE, values.shape[1]), axis=0)

    def add_rows(values):
        return jnp.sum(values, axis=0, keepdims=True)

    def start_exchange(which, one_tile=False):
        def send(step, carry):
            other = lax.rem(me + step, N)
            place = 0 if one_tile else pl.multiple_of(other * TILE, TILE)
            pltpu.make_async_remote_copy(
                src_ref=v.outgoing.at[which, pl.ds(place, TILE)],
                dst_ref=v.incoming.at[which, pl.ds(pl.multiple_of(me * TILE, TILE), TILE)],
                send_sem=v.give.at[which],
                recv_sem=v.take.at[which],
                device_id={"nodes": other},
                device_id_type=MESH,
            ).start()
            return carry

        lax.fori_loop(1, N, send, 0)
        own = pl.ds(pl.multiple_of(me * TILE, TILE), TILE)
        mine = pl.ds(0, TILE) if one_tile else own
        v.incoming[which, own, :] = v.outgoing[which, mine, :]

    def wait_bytes(ref, semaphore):
        pltpu.make_async_copy(ref, ref, semaphore).wait()

    def end_exchange(which):
        wait_bytes(v.incoming.at[which, pl.ds(0, (N - 1) * TILE)], v.take.at[which])

    def row_in_tile(rows):
        return lax.rem(iota((rows, D), 0), TILE)

    def with_sums(values, first, second):
        row = row_in_tile(values.shape[0])
        return values + jnp.where(row == z.send, first, 0.0) + jnp.where(row == z.send + 1, second, 0.0)

    def arrived_sums(which):
        tile = jnp.sum(v.incoming[which].reshape(N, TILE, D), axis=0)
        return tile[z.send : z.send + 1, :], tile[z.send + 1 : z.send + 2, :]

    def arrived_rows(which):
        values = v.incoming[which]
        return jnp.where(row_in_tile(z.halo) < z.send, values, 0.0)

    def give_rows_back(which):
        high, low = halves(arrived_rows(which))
        listed = v.list_t[:, : z.halo]
        return mm(listed, high) + mm(listed, low)

    def stage_copy(layer, first, stage, source, target, device):
        copy = pltpu.make_async_remote_copy(
            src_ref=source,
            dst_ref=target,
            send_sem=v.give_stage.at[layer, first, stage],
            recv_sem=v.take_stage.at[layer, first, stage],
            device_id=device,
            device_id_type=MESH,
        )
        copy.start()

    sends_to_end = []

    def stage_sent(layer, first, stage, ref):
        sends_to_end.append((ref, v.give_stage.at[layer, first, stage]))

    section_rows = pl.ds(pl.multiple_of(sec * z.share, TILE), z.share)

    def piece_rows(which):
        return pl.ds(pl.multiple_of(sec * z.share + which * z.piece, TILE), z.piece)

    def outer_device(which):
        return {"nodes": which * 2 + core}

    def start_stage(stage, layer, first, count):
        mats = pl.ds(first, count)
        if stage == CORE:
            stage_copy(
                layer,
                first,
                stage,
                v.sums.at[layer, mats, 1 - core],
                v.from_core.at[layer, mats],
                {"nodes": mate},
            )
            stage_sent(layer, first, stage, v.from_core.at[layer, mats])
        elif stage == SECTION:
            for step in range(1, S):
                other = lax.rem(sec + step, S)
                rows = pl.ds(pl.multiple_of(other * z.share, TILE), z.share)
                stage_copy(
                    layer,
                    first,
                    stage,
                    v.sums.at[layer, mats, core, rows],
                    v.from_section.at[layer, step - 1, mats],
                    {"section": other},
                )
            stage_sent(layer, first, stage, v.from_section.at[layer, :, mats])
        elif stage == OUTER:
            if z.owners == O:
                for step in range(1, O):
                    other = lax.rem(outer + step, O)
                    stage_copy(
                        layer,
                        first,
                        stage,
                        v.sums.at[layer, mats, core, piece_rows(other)],
                        v.from_outer.at[layer, step, mats],
                        outer_device(other),
                    )
                stage_sent(layer, first, stage, v.from_outer.at[layer, pl.ds(1, O - 1), mats])
            else:
                for other in range(z.owners):

                    @pl.when(outer != other)
                    def _():
                        stage_copy(
                            layer,
                            first,
                            stage,
                            v.sums.at[layer, mats, core, piece_rows(other)],
                            v.from_outer.at[layer, lax.rem(outer - other + O, O), mats],
                            outer_device(other),
                        )
                        wait_bytes(
                            v.from_outer.at[layer, 0, mats], v.give_stage.at[layer, first, stage]
                        )

        elif stage == OUTER_BACK:

            def send_all():
                for step in range(1, O):
                    stage_copy(
                        layer,
                        first,
                        stage,
                        v.whole.at[layer, mats, piece_rows(outer)],
                        v.whole.at[layer, mats, piece_rows(outer)],
                        outer_device(lax.rem(outer + step, O)),
                    )

            if z.owners == O:
                send_all()
                stage_sent(layer, first, stage, v.from_outer.at[layer, pl.ds(1, O - 1), mats])
            else:

                @pl.when(outer < z.owners)
                def _():
                    send_all()
                    wait_bytes(
                        v.from_outer.at[layer, pl.ds(1, O - 1), mats],
                        v.give_stage.at[layer, first, stage],
                    )

        elif stage == SECTION_BACK:
            for step in range(1, S):
                stage_copy(
                    layer,
                    first,
                    stage,
                    v.whole.at[layer, mats, section_rows],
                    v.whole.at[layer, mats, section_rows],
                    {"section": lax.rem(sec + step, S)},
                )
            stage_sent(layer, first, stage, v.from_section.at[layer, :, mats])
        elif stage == CORE_BACK:
            columns = pl.ds(pl.multiple_of(core * half, LANES), half)
            for mat in range(first, first + count):
                source = v.whole.at[layer, mat]
                target = grads_out[mat].at[layer, :, columns]
                pltpu.make_async_remote_copy(
                    src_ref=source,
                    dst_ref=target,
                    send_sem=v.give_back.at[layer, mat],
                    recv_sem=v.take_back.at[layer, mat],
                    device_id={"nodes": mate},
                    device_id_type=MESH,
                ).start()
                pltpu.make_async_copy(source, target, v.store.at[layer * 3 + mat]).start()

    def end_stage(stage, layer, first, count):
        mats = pl.ds(first, count)
        taken = v.take_stage.at[layer, first, stage]
        each = range(first, first + count)
        if stage == CORE:
            wait_bytes(v.from_core.at[layer, mats], taken)
            for mat in each:
                v.sums[layer, mat, core] = v.sums[layer, mat, core] + v.from_core[layer, mat]
        elif stage == SECTION:
            wait_bytes(v.from_section.at[layer, :, mats], taken)
            for mat in each:
                value = v.sums[layer, mat, core, section_rows, :]
                for step in range(S - 1):
                    value = value + v.from_section[layer, step, mat]
                v.sums[layer, mat, core, section_rows, :] = value
        elif stage == OUTER:

            def add():
                wait_bytes(v.from_outer.at[layer, pl.ds(1, O - 1), mats], taken)
                for mat in each:
                    value = v.sums[layer, mat, core, piece_rows(outer), :]
                    for step in range(1, O):
                        value = value + v.from_outer[layer, step, mat]
                    v.whole[layer, mat, piece_rows(outer), :] = value

            if z.owners == O:
                add()
            else:
                pl.when(outer < z.owners)(add)
        elif stage == OUTER_BACK:
            if z.owners == O:
                wait_bytes(v.from_outer.at[layer, pl.ds(1, O - 1), mats], taken)
            else:
                wait_bytes(v.from_outer.at[layer, pl.ds(1, z.owners - 1), mats], taken)

                @pl.when(outer >= z.owners)
                def _():
                    wait_bytes(v.from_outer.at[layer, 0, mats], taken)

        elif stage == SECTION_BACK:
            wait_bytes(v.from_section.at[layer, :, mats], taken)
        elif stage == CORE_BACK:
            columns = pl.ds(pl.multiple_of(core * half, LANES), half)
            for mat in each:
                source = v.whole.at[layer, mat]
                target = grads_out[mat].at[layer, :, columns]
                wait_bytes(source, v.give_back.at[layer, mat])
                wait_bytes(source, v.take_back.at[layer, mat])
                pltpu.make_async_copy(source, target, v.store.at[layer * 3 + mat]).wait()

    loads[1].wait()
    v.listed_row[...] = jnp.zeros_like(v.listed_row)
    v.listed_row[0:1, : z.listed] = v.listed_in[pl.ds(sec, 1), :].astype(F32)
    spread_from = iota((v.listed_row.shape[1], z.halo_pad), 0)
    spread_to = iota((v.listed_row.shape[1], z.halo_pad), 1)
    spread = as_ones(
        (lax.div(spread_from, z.send) == lax.div(spread_to, TILE))
        & (lax.rem(spread_from, z.send) == lax.rem(spread_to, TILE))
        & (spread_from < z.listed)
    )
    listed = mm(v.listed_row[...].astype(BF16), spread)[0:1, :]
    place = iota((1, z.halo_pad), 1)
    real = (lax.rem(place, TILE) < z.send) & (place < z.halo)
    listed = jnp.where(real, listed, -1.0)
    list_t = jnp.where(iota((R, z.halo_pad), 0).astype(F32) == listed, 1.0, 0.0)
    v.list_t[...] = list_t.astype(BF16)
    v.list[...] = list_t.T[: z.halo, :].astype(BF16)

    loads[0].wait()
    own = v.features_in[...]
    v.h[pl.ds(0, R), :] = own
    high, low = halves(own)
    v.h_hi[pl.ds(0, R), :] = high
    v.h_lo[pl.ds(0, R), :] = low
    v.outgoing[FEATURES] = mm(v.list[...], high) + mm(v.list[...], low)
    pl.semaphore_wait(barrier, N - 1 + S - 1)
    start_exchange(FEATURES)

    for load in loads[2:5]:
        load.wait()
    for layer in range(2):
        for mat in range(3):
            high, low = halves(v.weights_in[mat, layer])
            v.weights_hi[layer, mat] = high
            v.weights_lo[layer, mat] = low

    def weight(layer, mat):
        return v.weights_hi[layer, mat], v.weights_lo[layer, mat]

    for load in loads[5:11]:
        load.wait()
    named = v.slots_in[...]
    offset = named - R
    remote = R + lax.div(offset, z.send) * TILE + lax.rem(offset, z.send)
    named = jnp.where(named < R, named, remote).astype(F32)
    v.prep[...] = jnp.zeros_like(v.prep)
    v.prep[pl.ds(0, K), :] = named
    v.prep[pl.ds(K, 1), :] = v.degree_in[pl.ds(sec, 1), :].astype(F32)
    v.prep[pl.ds(K + 1, 1), :] = v.mask_in[pl.ds(sec, 1), :].astype(F32)
    v.prep_t[...] = v.prep[...].T
    for slot in range(1, K):
        column = v.prep_t[:, slot : slot + 1]
        v.pick[slot - 1] = as_ones(iota((R, T), 1).astype(F32) == column)
        row = v.prep[slot : slot + 1, :]
        v.pick_t[:, (slot - 1) * R : slot * R] = as_ones(iota((z.picked, R), 0).astype(F32) == row)
    group = D // HEADS
    block_row = lax.div(lax.rem(iota((2 * D, D), 0), D), group)
    v.ones[...] = as_ones(block_row == lax.div(iota((2 * D, D), 1), group))

    def project(layer):
        rows = pl.ds(0, R)
        own = (v.h_hi[rows, :], v.h_lo[rows, :])
        left = mm3(own, weight(layer, 0))
        v.taken[layer, 0] = left
        high, low = halves(left)
        v.table_hi[rows, :] = high
        v.table_lo[rows, :] = low
        v.right[layer] = mm3(own, weight(layer, 1))
        v.skip[...] = mm3(own, weight(layer, 2))

    def project_halo(layer):
        rows = pl.ds(R, z.halo_pad)
        left = mm3((v.h_hi[rows, :], v.h_lo[rows, :]), weight(layer, 0))
        high, low = halves(left)
        v.table_hi[rows, :] = high
        v.table_lo[rows, :] = low

    def store_halo(values):
        if z.halo < z.halo_pad:
            rest = pl.ds(R + z.halo, z.halo_pad - z.halo)
            v.h[rest, :] = jnp.zeros((z.halo_pad - z.halo, D), F32)
            v.h_hi[rest, :] = jnp.zeros((z.halo_pad - z.halo, D), BF16)
            v.h_lo[rest, :] = jnp.zeros((z.halo_pad - z.halo, D), BF16)
        rows = pl.ds(R, z.halo)
        v.h[rows, :] = values
        high, low = halves(values)
        v.h_hi[rows, :] = high
        v.h_lo[rows, :] = low

    def keep_transposed(layer):
        high, low = halves(v.h[...].T)
        v.ht_hi[layer] = high
        v.ht_lo[layer] = low

    def head_sums():
        def one(slot, carry):
            v.score[slot] = mm(v.pair[slot], v.ones[...])
            return carry

        lax.fori_loop(0, K, one, 0)

    def store_pair(slot, rows, values):
        high, low = halves(values)
        v.pair[slot, rows, pl.ds(0, D)] = high
        v.pair[slot, rows, pl.ds(D, D)] = low

    def attend(layer):
        def gather(slot, carry):
            pick = v.pick[slot - 1]
            v.taken[layer, slot] = mm(pick, v.table_hi[...]) + mm(pick, v.table_lo[...])
            return carry

        lax.fori_loop(1, K, gather, 0)
        vector = v.vector_in[layer : layer + 1, :]

        def activate(i, carry):
            rows = chunk(i)
            right = v.right[layer, rows, :]
            for slot in range(K):
                u = v.taken[layer, slot, rows, :] + right
                sig = 1.0 / (1.0 + jnp.exp(-u))
                v.sig[layer, slot, rows, :] = sig
                store_pair(slot, rows, u * sig * vector)
            return carry

        rows_loop(activate, 0)
        head_sums()

        def mix(i, carry):
            rows = chunk(i)
            count = jnp.broadcast_to(v.prep_t[rows, K : K + 1], (CHUNK, D))
            scores = [
                jnp.where(count > slot, v.score[slot, rows, :], MASKED_SCORE) for slot in range(K)
            ]
            highest = functools.reduce(jnp.maximum, scores)
            powers = [jnp.exp(score - highest) for score in scores]
            scale = 1.0 / functools.reduce(jnp.add, powers)
            joined = jnp.zeros((CHUNK, D), F32)
            for slot in range(K):
                alpha = powers[slot] * scale
                v.alpha[layer, slot, rows, :] = alpha
                joined = joined + alpha * v.taken[layer, slot, rows, :]
            v.joined[layer, rows, :] = joined
            mixed = joined + v.skip[rows, :]
            v.mixed[rows, :] = mixed
            return carry[0] + fold(mixed), carry[1] + fold(mixed * mixed)

        nothing = jnp.zeros((TILE, D), F32)
        first, second = rows_loop(mix, (nothing, nothing))
        return add_rows(first), add_rows(second)

    def moments(which):
        first, second = arrived_sums(which)
        mean = first / total_rows
        return mean, lax.rsqrt(second / total_rows - mean * mean + VARIANCE_EPS)

    def activation(layer, mixed, mean, inverse):
        normed = (mixed - mean) * inverse
        pre = v.gain_in[layer : layer + 1, :] * normed + v.shift_in[layer : layer + 1, :]
        power = jnp.exp(jnp.minimum(pre, 0.0))
        return normed, jnp.where(pre > 0, 1.0, power), jnp.where(pre > 0, pre, power - 1.0)

    def sums_tile(which, first, second):
        v.outgoing[which, pl.ds(0, TILE), :] = with_sums(jnp.zeros((TILE, D), F32), first, second)

    def list_rows(values):
        high, low = halves(values)
        return mm(v.list[...], high) + mm(v.list[...], low)

    project(0)
    end_exchange(FEATURES)
    store_halo(arrived_rows(FEATURES))
    project_halo(0)
    first, second = attend(0)
    v.outgoing[MIXED] = with_sums(list_rows(v.mixed[...]), first, second)
    start_exchange(MIXED)
    keep_transposed(0)
    end_exchange(MIXED)
    mean0, inverse0 = moments(MIXED)

    def finish0(i, carry):
        rows = chunk(i)
        normed, slope, hidden = activation(0, v.mixed[rows, :], mean0, inverse0)
        v.normed[0, rows, :] = normed
        v.slope[0, rows, :] = slope
        v.h[rows, :] = hidden
        high, low = halves(hidden)
        v.h_hi[rows, :] = high
        v.h_lo[rows, :] = low
        return carry

    rows_loop(finish0, 0)
    normed, slope, hidden = activation(0, arrived_rows(MIXED), mean0, inverse0)
    v.halo_normed[...] = normed
    v.halo_slope[...] = slope
    store_halo(jnp.where(row_in_tile(z.halo) < z.send, hidden, 0.0))

    project(1)
    project_halo(1)
    first, second = attend(1)
    sums_tile(SUMS, first, second)
    start_exchange(SUMS, True)
    keep_transposed(1)
    loads[11].wait()
    end_exchange(SUMS)
    mean1, inverse1 = moments(SUMS)

    def finish1(i, carry):
        rows = chunk(i)
        normed, slope, hidden = activation(1, v.mixed[rows, :], mean1, inverse1)
        v.normed[1, rows, :] = normed
        v.out_rows[rows, :] = hidden
        dpre = v.cotangent_in[rows, :] * v.prep_t[rows, K + 1 : K + 2] * slope
        v.dpre[rows, :] = dpre
        return carry[0] + fold(dpre), carry[1] + fold(dpre * normed)

    nothing = jnp.zeros((TILE, D), F32)
    first, second = rows_loop(finish1, (nothing, nothing))
    shift1, gain1 = add_rows(first), add_rows(second)
    sums_tile(BACK_SUMS, shift1, gain1)
    start_exchange(BACK_SUMS, True)
    out_copy = pltpu.make_async_copy(v.out_rows, out.at[0], v.store.at[6])
    out_copy.start()

    def normalization_back(layer, which, inverse):
        first, second = arrived_sums(which)
        first = first / total_rows
        second = second / total_rows
        scale = inverse * v.gain_in[layer : layer + 1, :]

        def one(i, carry):
            rows = chunk(i)
            dmixed = scale * (v.dpre[rows, :] - first - v.normed[layer, rows, :] * second)
            v.dmixed[rows, :] = dmixed
            high, low = halves(dmixed)
            v.dm_hi[rows, :] = high
            v.dm_lo[rows, :] = low
            return carry

        rows_loop(one, 0)

    def attend_back(layer, between=()):
        vector = v.vector_in[layer : layer + 1, :]

        def differences(i, carry):
            rows = chunk(i)
            joined = v.joined[layer, rows, :]
            dmixed = v.dmixed[rows, :]
            for slot in range(K):
                store_pair(slot, rows, (v.taken[layer, slot, rows, :] - joined) * dmixed)
            return carry

        rows_loop(differences, 0)
        head_sums()
        for step in between[:1]:
            step()

        def one(i, carry):
            rows = chunk(i)
            right = v.right[layer, rows, :]
            dmixed = v.dmixed[rows, :]
            dright = jnp.zeros((CHUNK, D), F32)
            for slot in range(K):
                u = v.taken[layer, slot, rows, :] + right
                sig = v.sig[layer, slot, rows, :]
                alpha = v.alpha[layer, slot, rows, :]
                dscore = alpha * v.score[slot, rows, :]
                carry = carry + fold(dscore * u * sig)
                du = dscore * vector * sig * (1.0 + u * (1.0 - sig))
                dright = dright + du
                dleft = du + alpha * dmixed
                if slot == 0:
                    v.dleft_self[rows, :] = dleft
                else:
                    high, low = halves(dleft)
                    place = pl.ds(pl.multiple_of((slot - 1) * R + i * CHUNK, CHUNK), CHUNK)
                    v.dleft_hi[place, :] = high
                    v.dleft_lo[place, :] = low
            high, low = halves(dright)
            v.dr_hi[rows, :] = high
            v.dr_lo[rows, :] = low
            return carry

        vector_sum = rows_loop(one, jnp.zeros((TILE, D), F32))
        for step in between[1:]:
            step()

        def scattered(rows):
            pick = v.pick_t[rows, :]
            return mm(pick, v.dleft_hi[...]) + mm(pick, v.dleft_lo[...])

        rows = pl.ds(0, R)
        high, low = halves(scattered(rows) + v.dleft_self[...])
        v.dl_hi[rows, :] = high
        v.dl_lo[rows, :] = low
        rows = pl.ds(R, z.halo)
        high, low = halves(scattered(rows))
        v.dl_hi[rows, :] = high
        v.dl_lo[rows, :] = low
        return add_rows(vector_sum)

    def dleft(rows):
        return v.dl_hi[rows, :], v.dl_lo[rows, :]

    def input_back(layer):
        own = pl.ds(0, R)
        v.dh[...] = (
            mm3(dleft(own), weight(layer, 0), mm_nt)
            + mm3((v.dr_hi[...], v.dr_lo[...]), weight(layer, 1), mm_nt)
            + mm3((v.dm_hi[...], v.dm_lo[...]), weight(layer, 2), mm_nt)
        )
        return mm3(dleft(pl.ds(R, z.halo)), weight(layer, 0), mm_nt)

    def weight_grad(layer, mat):
        if mat == 0:
            upstream = (v.dl_hi[...], v.dl_lo[...])
            inputs = (v.ht_hi[layer], v.ht_lo[layer])
        else:
            upstream = (v.dr_hi[...], v.dr_lo[...]) if mat == 1 else (v.dm_hi[...], v.dm_lo[...])
            inputs = (v.ht_hi[layer, :, pl.ds(0, R)], v.ht_lo[layer, :, pl.ds(0, R)])
        value = mm3(inputs, upstream)
        v.sums[layer, mat, 0] = value[:, :half]
        v.sums[layer, mat, 1] = value[:, half:]

    if z.halo < z.halo_pad:
        rest = pl.ds(R + z.halo, z.halo_pad - z.halo)
        v.dl_hi[rest, :] = jnp.zeros((z.halo_pad - z.halo, D), BF16)
        v.dl_lo[rest, :] = jnp.zeros((z.halo_pad - z.halo, D), BF16)

    end_exchange(BACK_SUMS)
    normalization_back(1, BACK_SUMS, inverse1)
    vector1 = attend_back(1)
    halo_back = input_back(1)
    dpre = v.dh[...] * v.slope[0]
    halo_dpre = halo_back * v.halo_slope[...]
    shift0 = add_rows(dpre) + add_rows(halo_dpre)
    gain0 = add_rows(dpre * v.normed[0]) + add_rows(halo_dpre * v.halo_normed[...])
    v.outgoing[BACK_ROWS] = with_sums(halo_back, shift0, gain0)
    start_exchange(BACK_ROWS)
    for mat in range(3):
        weight_grad(1, mat)
    start_stage(CORE, 1, 0, 3)
    end_exchange(BACK_ROWS)
    v.dpre[...] = (v.dh[...] + give_rows_back(BACK_ROWS)) * v.slope[0]

    normalization_back(0, BACK_ROWS, inverse0)
    end_stage(CORE, 1, 0, 3)
    start_stage(SECTION, 1, 0, 3)

    def step1():
        end_stage(SECTION, 1, 0, 3)
        start_stage(OUTER, 1, 0, 3)

    def step2():
        end_stage(OUTER, 1, 0, 3)
        start_stage(OUTER_BACK, 1, 0, 3)

    vector0 = attend_back(0, (step1, step2))
    for mat in range(3):
        weight_grad(0, mat)
    start_stage(CORE, 0, 0, 3)
    end_stage(OUTER_BACK, 1, 0, 3)
    start_stage(SECTION_BACK, 1, 0, 3)

    rows = (vector0, vector1, gain0, gain1, shift0, shift1)
    row = iota((TILE, D), 0)
    tile = jnp.zeros((TILE, D), F32)
    for place, value in enumerate(rows):
        tile = jnp.where(row == place, value, tile)
    v.outgoing[SMALL, pl.ds(0, TILE), :] = tile
    start_exchange(SMALL, True)

    halo_back = input_back(0)
    v.outgoing[INPUT_ROWS] = halo_back
    start_exchange(INPUT_ROWS)

    end_stage(CORE, 0, 0, 3)
    start_stage(SECTION, 0, 0, 3)
    end_exchange(SMALL)
    v.small[...] = jnp.sum(v.incoming[SMALL].reshape(N, TILE, D), axis=0)
    for step in range(1, S):
        pltpu.make_async_remote_copy(
            src_ref=v.small,
            dst_ref=v.small_in.at[step],
            send_sem=v.give_small.at[0],
            recv_sem=v.take_small.at[0],
            device_id={"section": lax.rem(sec + step, S)},
            device_id_type=MESH,
        ).start()
    end_stage(SECTION_BACK, 1, 0, 3)
    start_stage(CORE_BACK, 1, 0, 3)
    end_exchange(INPUT_ROWS)
    v.grad_rows[...] = v.dh[...] + give_rows_back(INPUT_ROWS)
    grad_copy = pltpu.make_async_copy(v.grad_rows, grad_in.at[0], v.store.at[7])
    grad_copy.start()
    end_stage(SECTION, 0, 0, 3)
    start_stage(OUTER, 0, 0, 3)
    wait_bytes(v.small_in.at[pl.ds(1, S - 1)], v.take_small.at[0])
    value = v.small[...]
    for step in range(1, S):
        value = value + v.small_in[step]
    last = []
    for place, (buffer, target) in enumerate(
        ((v.vector_out, g_vec), (v.gain_out, g_gain), (v.shift_out, g_shift))
    ):
        buffer[...] = value[2 * place : 2 * place + 2, :]
        copy = pltpu.make_async_copy(buffer, target, v.store.at[8 + place])
        copy.start()
        last.append(copy)
    end_stage(OUTER, 0, 0, 3)
    start_stage(OUTER_BACK, 0, 0, 3)
    end_stage(OUTER_BACK, 0, 0, 3)
    start_stage(SECTION_BACK, 0, 0, 3)
    end_stage(SECTION_BACK, 0, 0, 3)
    start_stage(CORE_BACK, 0, 0, 3)
    out_copy.wait()
    grad_copy.wait()
    for copy in last:
        copy.wait()
    for which in range(EXCHANGES):
        wait_bytes(v.outgoing.at[which, pl.ds(0, (N - 1) * TILE)], v.give.at[which])
    wait_bytes(v.small_in.at[pl.ds(1, S - 1)], v.give_small.at[0])
    for ref, semaphore in sends_to_end:
        wait_bytes(ref, semaphore)
    end_stage(CORE_BACK, 1, 0, 3)
    end_stage(CORE_BACK, 0, 0, 3)


def body(
    features,
    cotangent,
    train_mask,
    degree,
    neighbours,
    send_rows,
    w_left,
    w_right,
    w_res,
    attn_vec,
    bn_gain,
    bn_shift,
):
    batches, rows, width = features.shape
    sections = lax.axis_size("section")
    assert batches == sections
    z = sizes_of(
        sections, lax.axis_size("nodes"), rows, width, neighbours.shape[2], send_rows.shape[1]
    )
    shapes = scratch_of(z)
    shapes["mask_in"] = (train_mask.shape, jnp.int32)
    shapes["degree_in"] = (degree.shape, jnp.int32)
    shapes["listed_in"] = (send_rows.shape, jnp.int32)
    scratch = [pltpu.VMEM(shape, dtype) for shape, dtype in shapes.values()]
    scratch += [pltpu.SemaphoreType.DMA(shape) for shape in SEMAPHORES.values()]
    names = list(shapes) + list(SEMAPHORES)
    anywhere = pl.BlockSpec(memory_space=pl.ANY)
    square = jax.ShapeDtypeStruct((2, width, width), F32)
    columns = jax.ShapeDtypeStruct((2, width), F32)
    block = jax.ShapeDtypeStruct((1, rows, width), F32)
    return pl.pallas_call(
        functools.partial(kernel, z, names),
        out_shape=(block, block, square, square, square, columns, columns, columns),
        in_specs=[anywhere] * 12,
        out_specs=(anywhere,) * 8,
        scratch_shapes=scratch,
        compiler_params=pltpu.CompilerParams(
            collective_id=0, has_side_effects=True, vmem_limit_bytes=56 * 1024 * 1024
        ),
    )(
        features,
        cotangent,
        train_mask,
        degree,
        jnp.transpose(neighbours, (0, 2, 1)),
        send_rows,
        w_left,
        w_right,
        w_res,
        attn_vec,
        bn_gain,
        bn_shift,
    )


def solution(mesh):
    return jax.shard_map(
        body,
        mesh=mesh,
        in_specs=(
            P(None, "nodes", None),
            P(None, "nodes", None),
            P(None, "nodes"),
            P(None, "nodes"),
            P(None, "nodes", None),
            P(None, "nodes"),
            P(),
            P(),
            P(),
            P(),
            P(),
            P(),
        ),
        out_specs=(
            P("section", "nodes", None),
            P("section", "nodes", None),
            P(),
            P(),
            P(),
            P(),
            P(),
            P(),
        ),
        check_vma=False,
    )
```

time: 1150 us -> 94.8 us (0.08); the launches traced: 1130 us -> 94.5 us
  blocking collectives: 298 us -> 0 us
  local copies, waits for them, and re-layouts: 262 us -> 7.63 us
  other arithmetic: 213 us -> 0 us
  waiting for transfers between devices: 182 us -> 0 us
  starting transfers between devices: 92.4 us -> 0 us
  Pallas kernels: 0 us -> 86.2 us
  matrix products: 49.7 us -> 0 us
  loops' own time: 18.3 us -> 0 us
  between operations: 18.8 us -> 0.67 us
    psum x15 -> x0, blocking collectives: 298 us -> none  [the longest x7 121 us: body(): grad_sums = lax.psum(partial_value, 'nodes')]
    gather x42 -> x0, local copies, waits for them, and re-layouts: 163 us -> none  [the longest x28 154 us: attend(): picked = jnp.take(row_table, slot_index, axis=0)]
    scatter-add x14 -> x0, other arithmetic: 92.5 us -> none  [the longest x7 86.3 us: attend(): picked = jnp.take(row_table, slot_index, axis=0)]
    psum x1 -> x0, waiting for transfers between devices: 88 us -> none  [body(): lax.psum((layer_pick[:, None, None] * total_left, layer_pick[:, None, Non...]
    pallas_call x0 -> x1, Pallas kernels: none -> 86.2 us  [body(): pl.pallas_call(functools.partial(kernel, z, names), out_shape=(block, blo...]
    all_to_all x21 -> x0, starting transfers between devices: 73.2 us -> none  [the longest x14 49.8 us: body(): lax.all_to_all(jnp.take(left_rows, sending, axis=0), 'nodes', split_axis=...]
    ppermute x12 -> x0, waiting for transfers between devices: 63.1 us -> none  [passed_along(): return lax.ppermute(block, axis, route)]
    dot_general x77 -> x0, matrix products: 49.7 us -> none  [matmul(): jnp.dot(lhs_rows, rhs_rows, precision=PRECISE, preferred_element_type=jnp...]
  transfers between devices with their start and end apart: 36 -> 0, of which waited for: 20 -> 0; matrix products, arithmetic and copies ran while one was open for 16% -> 0% of each run, Pallas kernels for 0% -> 0%
where the time goes in v1:
time: 94.8 us; the launch traced here: 94.5 us
  Pallas kernels  86.2 us (91%)
  local copies, waits for them, and re-layouts  7.63 us (8%)
    pallas_call x1, Pallas kernels, body(): pl.pallas_call(functools.partial(kernel, z, names), out_shape=(block, blo...  86.2 us
    unnamed x22, local copies, waits for them, and re-layouts  7.63 us

profile of v1, /device:TPU:0, one launch (start us, length us, event | category | flops | bytes accessed | tf_op | source)
XLA Modules:
  0.0 94.5 jit_solution(484743214283594094)
XLA Ops:
  0.6 86.2 %shard_map.179 = (f32[1,256,256]{2,1,0:T(8,128)}, f32[1,256,256]{2,1,0:T(8,128)}, f32[2,256,256]{2,1,0:T(8,128)}, f32[2,256,256]{2,1,0:T(8,128)}, f32[2,256,256]...) custom-call(f32[4,256,256]{2,1,0:T(8,128)} %refs_0_.1, f32[4,256,256]{2,1,0:T(8,128)} %refs_1_.1, ...), custom_call_target="tpu_custom_call" | custom-call | tf_op jit(solution)/shard_map/pallas_call | solution.py:902
  86.8 0.0 copy-start.3
  86.8 0.0 copy-start.2
  86.8 1.7 %copy.28 = f32[1,256,256]{2,1,0:T(8,128)} copy(f32[1,256,256]{2,1,0:T(8,128)} %get-tuple-element.16) | data formatting | bytes 524288
  88.6 0.0 copy-done.3
  88.6 0.7 copy.29
  89.3 0.0 copy-done.2
  89.3 0.0 copy-start.1
  89.3 0.8 copy.30
  90.1 0.4 copy-done.1
  90.5 0.0 copy-start
  90.5 0.8 copy.31
  91.3 0.4 copy-done
  91.7 0.0 copy-start.6
  91.7 0.8 copy.32
  92.5 0.0 copy-done.6
  92.5 0.0 copy-start.5
  92.5 0.6 copy.33
  93.1 0.1 copy-done.5
  93.2 0.0 copy-start.4
  93.2 0.6 copy.34
  93.8 0.1 copy-done.4
  93.9 0.6 copy.35
Async XLA Ops:
  86.8 1.8 %copy-start.3 = (f32[1,256,256]{2,1,0:T(8,128)S(1)}, f32[1,256,256]{2,1,0:T(8,128)}, u32[]{:S(2)}) copy-start(f32[1,256,256]{2,1,0:T(8,128)} %get-tuple-element.17) | copy-start | bytes 786436
  86.8 2.5 %copy-start.2 = (f32[2,256,256]{2,1,0:T(8,128)S(1)}, f32[2,256,256]{2,1,0:T(8,128)}, u32[]{:S(2)}) copy-start(f32[2,256,256]{2,1,0:T(8,128)} %get-tuple-element.18) | copy-start | bytes 1572868
  89.3 1.2 %copy-start.1 = (f32[2,256,256]{2,1,0:T(8,128)S(1)}, f32[2,256,256]{2,1,0:T(8,128)}, u32[]{:S(2)}) copy-start(f32[2,256,256]{2,1,0:T(8,128)} %get-tuple-element.19) | copy-start | bytes 1572868
  90.5 1.2 %copy-start = (f32[2,256,256]{2,1,0:T(8,128)S(1)}, f32[2,256,256]{2,1,0:T(8,128)}, u32[]{:S(2)}) copy-start(f32[2,256,256]{2,1,0:T(8,128)} %get-tuple-element.20) | copy-start | bytes 1572868
  91.7 0.8 copy-start.6
  92.5 0.7 copy-start.5
  93.2 0.7 copy-start.4

commit v2 on v1

--- a/solution.py
+++ b/solution.py
@@ -14,6 +14,7 @@
 F32 = jnp.float32
 BF16 = jnp.bfloat16
 MESH = pl.DeviceIdType.MESH
+UNROLL = 4
 LANES = 128
 TILE = 8
 CHUNK = 16
@@ -203,7 +204,7 @@
         loads.append(copy)
 
     def rows_loop(body, start):
-        return lax.fori_loop(0, R // CHUNK, body, start)
+        return lax.fori_loop(0, R // CHUNK, body, start, unroll=UNROLL)
 
     def chunk(i):
         return pl.ds(pl.multiple_of(i * CHUNK, CHUNK), CHUNK)
@@ -213,6 +214,7 @@
 
     def add_rows(values):
         return jnp.sum(values, axis=0, keepdims=True)
+
 
     def start_exchange(which, one_tile=False):
         def send(step, carry):
@@ -440,6 +442,7 @@
                 wait_bytes(source, v.take_back.at[layer, mat])
                 pltpu.make_async_copy(source, target, v.store.at[layer * 3 + mat]).wait()
 
+
     loads[1].wait()
     v.listed_row[...] = jnp.zeros_like(v.listed_row)
     v.listed_row[0:1, : z.listed] = v.listed_in[pl.ds(sec, 1), :].astype(F32)
@@ -539,7 +542,7 @@
             v.score[slot] = mm(v.pair[slot], v.ones[...])
             return carry
 
-        lax.fori_loop(0, K, one, 0)
+        lax.fori_loop(0, K, one, 0, unroll=True)
 
     def store_pair(slot, rows, values):
         high, low = halves(values)
@@ -552,7 +555,7 @@
             v.taken[layer, slot] = mm(pick, v.table_hi[...]) + mm(pick, v.table_lo[...])
             return carry
 
-        lax.fori_loop(1, K, gather, 0)
+        lax.fori_loop(1, K, gather, 0, unroll=True)
         vector = v.vector_in[layer : layer + 1, :]
 
         def activate(i, carry):
@@ -731,14 +734,17 @@
             pick = v.pick_t[rows, :]
             return mm(pick, v.dleft_hi[...]) + mm(pick, v.dleft_lo[...])
 
-        rows = pl.ds(0, R)
-        high, low = halves(scattered(rows) + v.dleft_self[...])
-        v.dl_hi[rows, :] = high
-        v.dl_lo[rows, :] = low
-        rows = pl.ds(R, z.halo)
-        high, low = halves(scattered(rows))
-        v.dl_hi[rows, :] = high
-        v.dl_lo[rows, :] = low
+        def scatter():
+            rows = pl.ds(0, R)
+            high, low = halves(scattered(rows) + v.dleft_self[...])
+            v.dl_hi[rows, :] = high
+            v.dl_lo[rows, :] = low
+            rows = pl.ds(R, z.halo)
+            high, low = halves(scattered(rows))
+            v.dl_hi[rows, :] = high
+            v.dl_lo[rows, :] = low
+
+        scatter()
         return add_rows(vector_sum)
 
     def dleft(rows):
@@ -868,6 +874,14 @@
     end_stage(CORE_BACK, 0, 0, 3)
 
 
+def store_kernel(*refs):
+    copies = [pltpu.make_async_copy(refs[i], refs[8 + i], refs[16].at[i]) for i in range(8)]
+    for copy in copies:
+        copy.start()
+    for copy in copies:
+        copy.wait()
+
+
 def body(
     features,
     cotangent,
@@ -899,14 +913,16 @@
     square = jax.ShapeDtypeStruct((2, width, width), F32)
     columns = jax.ShapeDtypeStruct((2, width), F32)
     block = jax.ShapeDtypeStruct((1, rows, width), F32)
-    return pl.pallas_call(
+    results = (block, block, square, square, square, columns, columns, columns)
+    in_vmem = pl.BlockSpec(memory_space=pltpu.VMEM)
+    found = pl.pallas_call(
         functools.partial(kernel, z, names),
-        out_shape=(block, block, square, square, square, columns, columns, columns),
-        in_specs=[anywhere] * 12,
-        out_specs=(anywhere,) * 8,
+        out_shape=tuple(pltpu.VMEM(x.shape, x.dtype) for x in results),
+        in_specs=[pl.BlockSpec(memory_space=pltpu.HBM)] * 12,
+        out_specs=(in_vmem,) * 8,
         scratch_shapes=scratch,
         compiler_params=pltpu.CompilerParams(
-            collective_id=0, has_side_effects=True, vmem_limit_bytes=56 * 1024 * 1024
+            collective_id=0, has_side_effects=True, vmem_limit_bytes=60 * 1024 * 1024
         ),
     )(
         features,
@@ -922,6 +938,14 @@
         bn_gain,
         bn_shift,
     )
+    return pl.pallas_call(
+        store_kernel,
+        out_shape=results,
+        in_specs=[anywhere] * 8,
+        out_specs=(anywhere,) * 8,
+        scratch_shapes=[pltpu.SemaphoreType.DMA((8,))],
+        compiler_params=pltpu.CompilerParams(vmem_limit_bytes=1024 * 1024),
+    )(*found)
 
 
 def solution(mesh):

time: 94.8 us -> 80 us (0.84)
  local copies, waits for them, and re-layouts: 7.63 us -> 0 us
  Pallas kernels: 86.2 us -> 79.2 us
    unnamed x22 -> x0, local copies, waits for them, and re-layouts: 7.63 us -> none
    pallas_call x1 -> x2, Pallas kernels: 86.2 us -> 79.2 us  [the longest x1 77.8 us: body(): pl.pallas_call(functools.partial(kernel, z, names), out_shape=tuple((pltp...]
where the time goes in v2:
time: 80 us; the launch traced here: 79.8 us
  Pallas kernels  79.2 us (99%)
    pallas_call x1, Pallas kernels, body(): pl.pallas_call(functools.partial(kernel, z, names), out_shape=tuple((pltp...  77.8 us

profile of v2, /device:TPU:0, one launch (start us, length us, event | category | flops | bytes accessed | tf_op | source)
XLA Modules:
  0.0 79.8 jit_solution(10290911781870835991)
XLA Ops:
  0.6 77.8 %shard_map.179 = (f32[1,256,256]{2,1,0:T(8,128)S(1)}, f32[1,256,256]{2,1,0:T(8,128)S(1)}, f32[2,256,256]{2,1,0:T(8,128)S(1)}, f32[2,256,256]{2,1,0:T(8,128)S(1)}...) custom-call(f32[4,256,256]{2,1,0:T(8,128)} %refs_0_.1, ...), custom_call_target="tpu_custom_call" | custom-call | tf_op jit(solution)/shard_map/pallas_call | solution.py:918
  78.4 1.4 %shard_map.180 = (f32[1,256,256]{2,1,0:T(8,128)}, f32[1,256,256]{2,1,0:T(8,128)}, f32[2,256,256]{2,1,0:T(8,128)}, f32[2,256,256]{2,1,0:T(8,128)}, f32[2,256,256]...) custom-call(f32[1,256,256]{2,1,0:T(8,128)S(1)} %get-tuple-element.16.refs_0_, ...), custom_call_target="tpu_custom_call" | custom-call | tf_op jit(solution)/shard_map/pallas_call | solution.py:941

commit v3 on v2

--- a/solution.py
+++ b/solution.py
@@ -68,7 +68,6 @@
 def scratch_of(z):
     R, D, K, T = z.rows, z.width, z.slots, z.table
     S, O = z.sections, z.outer
-    half = D // 2
     vmem = {
         "features_in": ((R, D), F32),
         "cotangent_in": ((R, D), F32),
@@ -126,16 +125,10 @@
         "incoming": ((EXCHANGES, z.halo, D), F32),
         "small": ((TILE, D), F32),
         "small_in": ((S, TILE, D), F32),
-        "vector_out": ((2, D), F32),
-        "gain_out": ((2, D), F32),
-        "shift_out": ((2, D), F32),
-        "out_rows": ((R, D), F32),
-        "grad_rows": ((R, D), F32),
-        "sums": ((2, 3, 2, R, half), F32),
-        "from_core": ((2, 3, R, half), F32),
-        "from_section": ((2, S - 1, 3, z.share, half), F32),
-        "from_outer": ((2, O, 3, z.piece, half), F32),
-        "whole": ((2, 3, R, half), F32),
+        "sums": ((2, 3, R, D), F32),
+        "from_core": ((2, 3, R, D), F32),
+        "from_section": ((2, S - 1, 3, z.share, D), F32),
+        "from_outer": ((2, O, 3, z.piece, D), F32),
     }
     return vmem
 
@@ -148,21 +141,16 @@
     "take_small": (1,),
     "give_stage": (2, 3, STAGES),
     "take_stage": (2, 3, STAGES),
-    "give_back": (2, 3),
-    "take_back": (2, 3),
-    "store": (16,),
 }
 
 
 def kernel(z, names, *refs):
     features, cotangent, train_mask, degree, neighbours, send_rows = refs[:6]
     w_left, w_right, w_res, attn_vec, bn_gain, bn_shift = refs[6:12]
-    out, grad_in, g_left, g_right, g_res, g_vec, g_gain, g_shift = refs[12:20]
-    v = types.SimpleNamespace(**dict(zip(names, refs[20:])))
-    grads_out = (g_left, g_right, g_res)
+    out, grad_in, grads, g_vec, g_gain, g_shift = refs[12:18]
+    v = types.SimpleNamespace(**dict(zip(names, refs[18:])))
     R, D, K, T = z.rows, z.width, z.slots, z.table
     S, N, O = z.sections, z.partitions, z.outer
-    half = D // 2
     total_rows = R * N
     sec = lax.axis_index("section")
     me = lax.axis_index("nodes")
@@ -261,23 +249,26 @@
         listed = v.list_t[:, : z.halo]
         return mm(listed, high) + mm(listed, low)
 
+    sends_to_end = []
+
+    def on(which, body):
+        pl.when(core == which)(body)
+
     def stage_copy(layer, first, stage, source, target, device):
-        copy = pltpu.make_async_remote_copy(
+        pltpu.make_async_remote_copy(
             src_ref=source,
             dst_ref=target,
             send_sem=v.give_stage.at[layer, first, stage],
             recv_sem=v.take_stage.at[layer, first, stage],
             device_id=device,
             device_id_type=MESH,
-        )
-        copy.start()
-
-    sends_to_end = []
-
-    def stage_sent(layer, first, stage, ref):
-        sends_to_end.append((ref, v.give_stage.at[layer, first, stage]))
-
-    section_rows = pl.ds(pl.multiple_of(sec * z.share, TILE), z.share)
+        ).start()
+
+    def stage_sent(layer, first, stage, ref, which):
+        sends_to_end.append((ref, lambda: v.give_stage.at[layer, first, stage], which))
+
+    def share_rows(which):
+        return pl.ds(pl.multiple_of(which * z.share, TILE), z.share)
 
     def piece_rows(which):
         return pl.ds(pl.multiple_of(sec * z.share + which * z.piece, TILE), z.piece)
@@ -285,31 +276,32 @@
     def outer_device(which):
         return {"nodes": which * 2 + core}
 
+    def from_others(layer, mats, count):
+        return v.from_outer.at[layer, pl.ds(1, count), mats]
+
+    def start_core(layer, mat):
+        on(
+            0,
+            lambda: stage_copy(
+                layer, mat, CORE, v.sums.at[layer, mat], v.from_core.at[layer, mat], {"nodes": mate}
+            ),
+        )
+        stage_sent(layer, mat, CORE, lambda: v.from_core.at[layer, mat], 0)
+
     def start_stage(stage, layer, first, count):
         mats = pl.ds(first, count)
-        if stage == CORE:
-            stage_copy(
-                layer,
-                first,
-                stage,
-                v.sums.at[layer, mats, 1 - core],
-                v.from_core.at[layer, mats],
-                {"nodes": mate},
-            )
-            stage_sent(layer, first, stage, v.from_core.at[layer, mats])
-        elif stage == SECTION:
+        if stage == SECTION:
             for step in range(1, S):
                 other = lax.rem(sec + step, S)
-                rows = pl.ds(pl.multiple_of(other * z.share, TILE), z.share)
                 stage_copy(
                     layer,
                     first,
                     stage,
-                    v.sums.at[layer, mats, core, rows],
+                    v.sums.at[layer, mats, share_rows(other)],
                     v.from_section.at[layer, step - 1, mats],
                     {"section": other},
                 )
-            stage_sent(layer, first, stage, v.from_section.at[layer, :, mats])
+            stage_sent(layer, first, stage, lambda: v.from_section.at[layer, :, mats], 1)
         elif stage == OUTER:
             if z.owners == O:
                 for step in range(1, O):
@@ -318,11 +310,11 @@
                         layer,
                         first,
                         stage,
-                        v.sums.at[layer, mats, core, piece_rows(other)],
+                        v.sums.at[layer, mats, piece_rows(other)],
                         v.from_outer.at[layer, step, mats],
                         outer_device(other),
                     )
-                stage_sent(layer, first, stage, v.from_outer.at[layer, pl.ds(1, O - 1), mats])
+                stage_sent(layer, first, stage, lambda: from_others(layer, mats, O - 1), 1)
             else:
                 for other in range(z.owners):
 
@@ -332,7 +324,7 @@
                             layer,
                             first,
                             stage,
-                            v.sums.at[layer, mats, core, piece_rows(other)],
+                            v.sums.at[layer, mats, piece_rows(other)],
                             v.from_outer.at[layer, lax.rem(outer - other + O, O), mats],
                             outer_device(other),
                         )
@@ -348,22 +340,21 @@
                         layer,
                         first,
                         stage,
-                        v.whole.at[layer, mats, piece_rows(outer)],
-                        v.whole.at[layer, mats, piece_rows(outer)],
+                        grads.at[layer, mats, piece_rows(outer)],
+                        grads.at[layer, mats, piece_rows(outer)],
                         outer_device(lax.rem(outer + step, O)),
                     )
 
             if z.owners == O:
                 send_all()
-                stage_sent(layer, first, stage, v.from_outer.at[layer, pl.ds(1, O - 1), mats])
+                stage_sent(layer, first, stage, lambda: from_others(layer, mats, O - 1), 1)
             else:
 
                 @pl.when(outer < z.owners)
                 def _():
                     send_all()
                     wait_bytes(
-                        v.from_outer.at[layer, pl.ds(1, O - 1), mats],
-                        v.give_stage.at[layer, first, stage],
+                        from_others(layer, mats, O - 1), v.give_stage.at[layer, first, stage]
                     )
 
         elif stage == SECTION_BACK:
@@ -372,50 +363,40 @@
                     layer,
                     first,
                     stage,
-                    v.whole.at[layer, mats, section_rows],
-                    v.whole.at[layer, mats, section_rows],
+                    grads.at[layer, mats, share_rows(sec)],
+                    grads.at[layer, mats, share_rows(sec)],
                     {"section": lax.rem(sec + step, S)},
                 )
-            stage_sent(layer, first, stage, v.from_section.at[layer, :, mats])
+            stage_sent(layer, first, stage, lambda: v.from_section.at[layer, :, mats], 1)
         elif stage == CORE_BACK:
-            columns = pl.ds(pl.multiple_of(core * half, LANES), half)
-            for mat in range(first, first + count):
-                source = v.whole.at[layer, mat]
-                target = grads_out[mat].at[layer, :, columns]
-                pltpu.make_async_remote_copy(
-                    src_ref=source,
-                    dst_ref=target,
-                    send_sem=v.give_back.at[layer, mat],
-                    recv_sem=v.take_back.at[layer, mat],
-                    device_id={"nodes": mate},
-                    device_id_type=MESH,
-                ).start()
-                pltpu.make_async_copy(source, target, v.store.at[layer * 3 + mat]).start()
+            stage_copy(
+                layer, first, stage, grads.at[layer, mats], grads.at[layer, mats], {"nodes": mate}
+            )
+            stage_sent(layer, first, stage, lambda: grads.at[layer, mats], 1)
 
     def end_stage(stage, layer, first, count):
         mats = pl.ds(first, count)
         taken = v.take_stage.at[layer, first, stage]
         each = range(first, first + count)
         if stage == CORE:
-            wait_bytes(v.from_core.at[layer, mats], taken)
-            for mat in each:
-                v.sums[layer, mat, core] = v.sums[layer, mat, core] + v.from_core[layer, mat]
+            wait_bytes(v.from_core.at[layer, first], taken)
+            v.sums[layer, first] = v.sums[layer, first] + v.from_core[layer, first]
         elif stage == SECTION:
             wait_bytes(v.from_section.at[layer, :, mats], taken)
             for mat in each:
-                value = v.sums[layer, mat, core, section_rows, :]
+                value = v.sums[layer, mat, share_rows(sec), :]
                 for step in range(S - 1):
                     value = value + v.from_section[layer, step, mat]
-                v.sums[layer, mat, core, section_rows, :] = value
+                v.sums[layer, mat, share_rows(sec), :] = value
         elif stage == OUTER:
 
             def add():
-                wait_bytes(v.from_outer.at[layer, pl.ds(1, O - 1), mats], taken)
+                wait_bytes(from_others(layer, mats, O - 1), taken)
                 for mat in each:
-                    value = v.sums[layer, mat, core, piece_rows(outer), :]
+                    value = v.sums[layer, mat, piece_rows(outer), :]
                     for step in range(1, O):
                         value = value + v.from_outer[layer, step, mat]
-                    v.whole[layer, mat, piece_rows(outer), :] = value
+                    grads[layer, mat, piece_rows(outer), :] = value
 
             if z.owners == O:
                 add()
@@ -423,9 +404,9 @@
                 pl.when(outer < z.owners)(add)
         elif stage == OUTER_BACK:
             if z.owners == O:
-                wait_bytes(v.from_outer.at[layer, pl.ds(1, O - 1), mats], taken)
+                wait_bytes(from_others(layer, mats, O - 1), taken)
             else:
-                wait_bytes(v.from_outer.at[layer, pl.ds(1, z.owners - 1), mats], taken)
+                wait_bytes(from_others(layer, mats, z.owners - 1), taken)
 
                 @pl.when(outer >= z.owners)
                 def _():
@@ -434,13 +415,19 @@
         elif stage == SECTION_BACK:
             wait_bytes(v.from_section.at[layer, :, mats], taken)
         elif stage == CORE_BACK:
-            columns = pl.ds(pl.multiple_of(core * half, LANES), half)
-            for mat in each:
-                source = v.whole.at[layer, mat]
-                target = grads_out[mat].at[layer, :, columns]
-                wait_bytes(source, v.give_back.at[layer, mat])
-                wait_bytes(source, v.take_back.at[layer, mat])
-                pltpu.make_async_copy(source, target, v.store.at[layer * 3 + mat]).wait()
+            wait_bytes(grads.at[layer, mats], taken)
+
+    def advance(*moves):
+        def run():
+            for stage, layer, first, count in moves:
+                if stage == CORE:
+                    for mat in range(first, first + count):
+                        end_stage(CORE, layer, mat, 1)
+                else:
+                    end_stage(stage, layer, first, count)
+                start_stage(stage + 1, layer, first, count)
+
+        on(1, run)
 
 
     loads[1].wait()
@@ -654,7 +641,7 @@
         rows = chunk(i)
         normed, slope, hidden = activation(1, v.mixed[rows, :], mean1, inverse1)
         v.normed[1, rows, :] = normed
-        v.out_rows[rows, :] = hidden
+        out[0, rows, :] = hidden
         dpre = v.cotangent_in[rows, :] * v.prep_t[rows, K + 1 : K + 2] * slope
         v.dpre[rows, :] = dpre
         return carry[0] + fold(dpre), carry[1] + fold(dpre * normed)
@@ -664,8 +651,6 @@
     shift1, gain1 = add_rows(first), add_rows(second)
     sums_tile(BACK_SUMS, shift1, gain1)
     start_exchange(BACK_SUMS, True)
-    out_copy = pltpu.make_async_copy(v.out_rows, out.at[0], v.store.at[6])
-    out_copy.start()
 
     def normalization_back(layer, which, inverse):
         first, second = arrived_sums(which)
@@ -684,7 +669,7 @@
 
         rows_loop(one, 0)
 
-    def attend_back(layer, between=()):
+    def attend_back(layer, between=None):
         vector = v.vector_in[layer : layer + 1, :]
 
         def differences(i, carry):
@@ -697,8 +682,6 @@
 
         rows_loop(differences, 0)
         head_sums()
-        for step in between[:1]:
-            step()
 
         def one(i, carry):
             rows = chunk(i)
@@ -727,8 +710,8 @@
             return carry
 
         vector_sum = rows_loop(one, jnp.zeros((TILE, D), F32))
-        for step in between[1:]:
-            step()
+        if between is not None:
+            between()
 
         def scattered(rows):
             pick = v.pick_t[rows, :]
@@ -766,9 +749,8 @@
         else:
             upstream = (v.dr_hi[...], v.dr_lo[...]) if mat == 1 else (v.dm_hi[...], v.dm_lo[...])
             inputs = (v.ht_hi[layer, :, pl.ds(0, R)], v.ht_lo[layer, :, pl.ds(0, R)])
-        value = mm3(inputs, upstream)
-        v.sums[layer, mat, 0] = value[:, :half]
-        v.sums[layer, mat, 1] = value[:, half:]
+        v.sums[layer, mat] = mm3(inputs, upstream)
+        start_core(layer, mat)
 
     if z.halo < z.halo_pad:
         rest = pl.ds(R + z.halo, z.halo_pad - z.halo)
@@ -785,45 +767,28 @@
     gain0 = add_rows(dpre * v.normed[0]) + add_rows(halo_dpre * v.halo_normed[...])
     v.outgoing[BACK_ROWS] = with_sums(halo_back, shift0, gain0)
     start_exchange(BACK_ROWS)
-    for mat in range(3):
+    for mat in (2, 1, 0):
         weight_grad(1, mat)
-    start_stage(CORE, 1, 0, 3)
+    advance((CORE, 1, 0, 3))
     end_exchange(BACK_ROWS)
     v.dpre[...] = (v.dh[...] + give_rows_back(BACK_ROWS)) * v.slope[0]
 
     normalization_back(0, BACK_ROWS, inverse0)
-    end_stage(CORE, 1, 0, 3)
-    start_stage(SECTION, 1, 0, 3)
-
-    def step1():
-        end_stage(SECTION, 1, 0, 3)
-        start_stage(OUTER, 1, 0, 3)
-
-    def step2():
-        end_stage(OUTER, 1, 0, 3)
-        start_stage(OUTER_BACK, 1, 0, 3)
-
-    vector0 = attend_back(0, (step1, step2))
-    for mat in range(3):
-        weight_grad(0, mat)
-    start_stage(CORE, 0, 0, 3)
-    end_stage(OUTER_BACK, 1, 0, 3)
-    start_stage(SECTION_BACK, 1, 0, 3)
-
-    rows = (vector0, vector1, gain0, gain1, shift0, shift1)
+    weight_grad(0, 2)
+    vector0 = attend_back(0, lambda: weight_grad(0, 1))
+    weight_grad(0, 0)
+
     row = iota((TILE, D), 0)
     tile = jnp.zeros((TILE, D), F32)
-    for place, value in enumerate(rows):
+    for place, value in enumerate((vector0, vector1, gain0, gain1, shift0, shift1)):
         tile = jnp.where(row == place, value, tile)
     v.outgoing[SMALL, pl.ds(0, TILE), :] = tile
     start_exchange(SMALL, True)
-
+    advance((CORE, 0, 1, 2))
     halo_back = input_back(0)
     v.outgoing[INPUT_ROWS] = halo_back
     start_exchange(INPUT_ROWS)
-
-    end_stage(CORE, 0, 0, 3)
-    start_stage(SECTION, 0, 0, 3)
+    advance((SECTION, 1, 0, 3), (CORE, 0, 0, 1), (SECTION, 0, 1, 2))
     end_exchange(SMALL)
     v.small[...] = jnp.sum(v.incoming[SMALL].reshape(N, TILE, D), axis=0)
     for step in range(1, S):
@@ -835,47 +800,46 @@
             device_id={"section": lax.rem(sec + step, S)},
             device_id_type=MESH,
         ).start()
-    end_stage(SECTION_BACK, 1, 0, 3)
-    start_stage(CORE_BACK, 1, 0, 3)
+    advance((OUTER, 1, 0, 3), (SECTION, 0, 0, 1), (OUTER, 0, 1, 2))
     end_exchange(INPUT_ROWS)
-    v.grad_rows[...] = v.dh[...] + give_rows_back(INPUT_ROWS)
-    grad_copy = pltpu.make_async_copy(v.grad_rows, grad_in.at[0], v.store.at[7])
-    grad_copy.start()
-    end_stage(SECTION, 0, 0, 3)
-    start_stage(OUTER, 0, 0, 3)
+    grad_in[0] = v.dh[...] + give_rows_back(INPUT_ROWS)
+    advance((OUTER_BACK, 1, 0, 3), (OUTER, 0, 0, 1), (OUTER_BACK, 0, 1, 2))
     wait_bytes(v.small_in.at[pl.ds(1, S - 1)], v.take_small.at[0])
     value = v.small[...]
     for step in range(1, S):
         value = value + v.small_in[step]
-    last = []
-    for place, (buffer, target) in enumerate(
-        ((v.vector_out, g_vec), (v.gain_out, g_gain), (v.shift_out, g_shift))
-    ):
-        buffer[...] = value[2 * place : 2 * place + 2, :]
-        copy = pltpu.make_async_copy(buffer, target, v.store.at[8 + place])
-        copy.start()
-        last.append(copy)
-    end_stage(OUTER, 0, 0, 3)
-    start_stage(OUTER_BACK, 0, 0, 3)
-    end_stage(OUTER_BACK, 0, 0, 3)
-    start_stage(SECTION_BACK, 0, 0, 3)
-    end_stage(SECTION_BACK, 0, 0, 3)
-    start_stage(CORE_BACK, 0, 0, 3)
-    out_copy.wait()
-    grad_copy.wait()
-    for copy in last:
-        copy.wait()
+    g_vec[...] = value[0:2, :]
+    g_gain[...] = value[2:4, :]
+    g_shift[...] = value[4:6, :]
+    advance((SECTION_BACK, 1, 0, 3), (OUTER_BACK, 0, 0, 1), (SECTION_BACK, 0, 1, 2))
+    advance((SECTION_BACK, 0, 0, 1))
+
+    def receive():
+        end_stage(CORE_BACK, 1, 0, 3)
+        end_stage(CORE_BACK, 0, 1, 2)
+        end_stage(CORE_BACK, 0, 0, 1)
+
+    on(0, receive)
     for which in range(EXCHANGES):
         wait_bytes(v.outgoing.at[which, pl.ds(0, (N - 1) * TILE)], v.give.at[which])
     wait_bytes(v.small_in.at[pl.ds(1, S - 1)], v.give_small.at[0])
-    for ref, semaphore in sends_to_end:
-        wait_bytes(ref, semaphore)
-    end_stage(CORE_BACK, 1, 0, 3)
-    end_stage(CORE_BACK, 0, 0, 3)
+
+    def sent(which):
+        for ref, semaphore, sender in sends_to_end:
+            if sender == which:
+                wait_bytes(ref(), semaphore())
+
+    on(0, lambda: sent(0))
+    on(1, lambda: sent(1))
 
 
 def store_kernel(*refs):
-    copies = [pltpu.make_async_copy(refs[i], refs[8 + i], refs[16].at[i]) for i in range(8)]
+    out, grad_in, grads, g_vec, g_gain, g_shift = refs[:6]
+    pairs = [(out, refs[6]), (grad_in, refs[7])]
+    for mat in range(3):
+        pairs += [(grads.at[layer, mat], refs[8 + mat].at[layer]) for layer in range(2)]
+    pairs += [(g_vec, refs[11]), (g_gain, refs[12]), (g_shift, refs[13])]
+    copies = [pltpu.make_async_copy(*pair, refs[14].at[i]) for i, pair in enumerate(pairs)]
     for copy in copies:
         copy.start()
     for copy in copies:
@@ -915,11 +879,13 @@
     block = jax.ShapeDtypeStruct((1, rows, width), F32)
     results = (block, block, square, square, square, columns, columns, columns)
     in_vmem = pl.BlockSpec(memory_space=pltpu.VMEM)
+    squares = jax.ShapeDtypeStruct((2, 3, width, width), F32)
+    kept = (block, block, squares, columns, columns, columns)
     found = pl.pallas_call(
         functools.partial(kernel, z, names),
-        out_shape=tuple(pltpu.VMEM(x.shape, x.dtype) for x in results),
+        out_shape=tuple(pltpu.VMEM(x.shape, x.dtype) for x in kept),
         in_specs=[pl.BlockSpec(memory_space=pltpu.HBM)] * 12,
-        out_specs=(in_vmem,) * 8,
+        out_specs=(in_vmem,) * 6,
         scratch_shapes=scratch,
         compiler_params=pltpu.CompilerParams(
             collective_id=0, has_side_effects=True, vmem_limit_bytes=60 * 1024 * 1024
@@ -941,9 +907,9 @@
     return pl.pallas_call(
         store_kernel,
         out_shape=results,
-        in_specs=[anywhere] * 8,
+        in_specs=[anywhere] * 6,
         out_specs=(anywhere,) * 8,
-        scratch_shapes=[pltpu.SemaphoreType.DMA((8,))],
+        scratch_shapes=[pltpu.SemaphoreType.DMA((11,))],
         compiler_params=pltpu.CompilerParams(vmem_limit_bytes=1024 * 1024),
     )(*found)
 

time: 80 us -> 68.7 us (0.86)
  Pallas kernels: 79.2 us -> 67.9 us
    pallas_call x1, Pallas kernels: 77.8 us -> 66.5 us  [body(): pl.pallas_call(functools.partial(kernel, z, names), out_shape=tuple((pltp...]
where the time goes in v3:
time: 68.7 us; the launch traced here: 68.5 us
  Pallas kernels  67.9 us (99%)
    pallas_call x1, Pallas kernels, body(): pl.pallas_call(functools.partial(kernel, z, names), out_shape=tuple((pltp...  66.5 us
    pallas_call x1, Pallas kernels, body(): pl.pallas_call(store_kernel, out_shape=results, in_specs=[anywhere] * 6,...  1.41 us

profile of v3, /device:TPU:0, one launch (start us, length us, event | category | flops | bytes accessed | tf_op | source)
XLA Modules:
  0.0 68.5 jit_solution(11792994062036119207)
XLA Ops:
  0.6 66.5 %shard_map.179 = (f32[1,256,256]{2,1,0:T(8,128)S(1)}, f32[1,256,256]{2,1,0:T(8,128)S(1)}, f32[2,3,256,256]{3,2,1,0:T(8,128)S(1)}, f32[2,256]{1,0:T(2,128)S(1)}, ...) custom-call(f32[4,256,256]{2,1,0:T(8,128)} %refs_0_.1, f32[4,256,256]{2,1,0:T(8,128)} %refs_1_.1, s32[4,256]{1,0:T(4,128)} %refs_2_.1, ...), custom_call_target="tpu_custom_call" | custom-call | tf_op jit(solution)/shard_map/pallas_call | solution.py:884
  67.1 1.4 %shard_map.180 = (f32[1,256,256]{2,1,0:T(8,128)}, f32[1,256,256]{2,1,0:T(8,128)}, f32[2,256,256]{2,1,0:T(8,128)}, f32[2,256,256]{2,1,0:T(8,128)}, f32[2,256,256]...) custom-call(f32[1,256,256]{2,1,0:T(8,128)S(1)} %get-tuple-element.14.refs_0_, ...), custom_call_target="tpu_custom_call" | custom-call | tf_op jit(solution)/shard_map/pallas_call | solution.py:907

commit v4 on v3

--- a/solution.py
+++ b/solution.py
@@ -15,12 +15,14 @@
 BF16 = jnp.bfloat16
 MESH = pl.DeviceIdType.MESH
 UNROLL = 4
+SHARED = ()
 LANES = 128
+GROUP = 64
 TILE = 8
 CHUNK = 16
 
-FEATURES, MIXED, SUMS, BACK_SUMS, BACK_ROWS, INPUT_ROWS, SMALL = range(7)
-EXCHANGES = 7
+FEATURES, MIXED, SUMS, BACK_SUMS, BACK_ROWS = range(5)
+EXCHANGES = 5
 CORE, SECTION, OUTER, OUTER_BACK, SECTION_BACK, CORE_BACK = range(6)
 STAGES = 6
 
@@ -44,6 +46,10 @@
 
 def iota(shape, dim):
     return lax.broadcasted_iota(jnp.int32, shape, dim)
+
+
+def sigmoid(u):
+    return 0.5 * jnp.tanh(0.5 * u) + 0.5
 
 
 def as_ones(condition):
@@ -84,7 +90,7 @@
         "prep": ((LANES, R), F32),
         "prep_t": ((R, LANES), F32),
         "listed_row": ((TILE, max(LANES, z.listed)), F32),
-        "pick": ((K - 1, R, T), BF16),
+        "pick": ((K - 1, R, R + 2 * z.halo_pad), BF16),
         "pick_t": ((z.picked, (K - 1) * R), BF16),
         "list": ((z.halo, R), BF16),
         "list_t": ((R, z.halo_pad), BF16),
@@ -94,10 +100,12 @@
         "h_lo": ((T, D), BF16),
         "ht_hi": ((2, D, T), BF16),
         "ht_lo": ((2, D, T), BF16),
-        "table_hi": ((T, D), BF16),
-        "table_lo": ((T, D), BF16),
+        "table_hi": ((R, D), BF16),
+        "table_lo": ((R, D), BF16),
+        "halo_table": ((2 * z.halo_pad, D), BF16),
         "taken": ((2, K, R, D), F32),
-        "sig": ((2, K, R, D), F32),
+        "act": ((2, K, R, D), F32),
+        "rise": ((2, K, R, D), F32),
         "alpha": ((2, K, R, D), F32),
         "joined": ((2, R, D), F32),
         "right": ((2, R, D), F32),
@@ -123,12 +131,17 @@
         "dh": ((R, D), F32),
         "outgoing": ((EXCHANGES, z.halo, D), F32),
         "incoming": ((EXCHANGES, z.halo, D), F32),
-        "small": ((TILE, D), F32),
-        "small_in": ((S, TILE, D), F32),
+        "small": ((4, TILE, D), F32),
+        "small_core": ((2, TILE, D), F32),
+        "small_outer": ((O, TILE, D), F32),
+        "small_section": ((S, TILE, D), F32),
+        "returning": ((z.halo, LANES), F32),
+        "returned": ((z.halo, LANES), F32),
         "sums": ((2, 3, R, D), F32),
         "from_core": ((2, 3, R, D), F32),
         "from_section": ((2, S - 1, 3, z.share, D), F32),
         "from_outer": ((2, O, 3, z.piece, D), F32),
+        "shares": ((3, O, z.share, D), F32),
     }
     return vmem
 
@@ -137,8 +150,10 @@
     "load": (12,),
     "give": (EXCHANGES,),
     "take": (EXCHANGES,),
-    "give_small": (1,),
-    "take_small": (1,),
+    "give_small": (4,),
+    "take_small": (4,),
+    "give_rows": (1,),
+    "take_rows": (1,),
     "give_stage": (2, 3, STAGES),
     "take_stage": (2, 3, STAGES),
 }
@@ -227,6 +242,9 @@
         pltpu.make_async_copy(ref, ref, semaphore).wait()
 
     def end_exchange(which):
+        wait_exchange(which)
+
+    def wait_exchange(which):
         wait_bytes(v.incoming.at[which, pl.ds(0, (N - 1) * TILE)], v.take.at[which])
 
     def row_in_tile(rows):
@@ -248,6 +266,9 @@
         high, low = halves(arrived_rows(which))
         listed = v.list_t[:, : z.halo]
         return mm(listed, high) + mm(listed, low)
+
+    def owner(layer):
+        return 1 - layer
 
     sends_to_end = []
 
@@ -281,12 +302,12 @@
 
     def start_core(layer, mat):
         on(
-            0,
+            1 - owner(layer),
             lambda: stage_copy(
                 layer, mat, CORE, v.sums.at[layer, mat], v.from_core.at[layer, mat], {"nodes": mate}
             ),
         )
-        stage_sent(layer, mat, CORE, lambda: v.from_core.at[layer, mat], 0)
+        stage_sent(layer, mat, CORE, lambda: v.from_core.at[layer, mat], 1 - owner(layer))
 
     def start_stage(stage, layer, first, count):
         mats = pl.ds(first, count)
@@ -301,7 +322,19 @@
                     v.from_section.at[layer, step - 1, mats],
                     {"section": other},
                 )
-            stage_sent(layer, first, stage, lambda: v.from_section.at[layer, :, mats], 1)
+            stage_sent(layer, first, stage, lambda: v.from_section.at[layer, :, mats], owner(layer))
+        elif stage == OUTER and layer in SHARED:
+            for step in range(1, O):
+                stage_copy(
+                    layer,
+                    first,
+                    stage,
+                    v.sums.at[layer, first, share_rows(sec)],
+                    v.shares.at[first, outer],
+                    outer_device(lax.rem(outer + step, O)),
+                )
+            stage_sent(layer, first, stage, lambda: v.shares.at[first, pl.ds(1, O - 1)], owner(layer))
+            v.shares[first, outer] = v.sums[layer, first, share_rows(sec), :]
         elif stage == OUTER:
             if z.owners == O:
                 for step in range(1, O):
@@ -314,7 +347,7 @@
                         v.from_outer.at[layer, step, mats],
                         outer_device(other),
                     )
-                stage_sent(layer, first, stage, lambda: from_others(layer, mats, O - 1), 1)
+                stage_sent(layer, first, stage, lambda: from_others(layer, mats, O - 1), owner(layer))
             else:
                 for other in range(z.owners):
 
@@ -347,7 +380,7 @@
 
             if z.owners == O:
                 send_all()
-                stage_sent(layer, first, stage, lambda: from_others(layer, mats, O - 1), 1)
+                stage_sent(layer, first, stage, lambda: from_others(layer, mats, O - 1), owner(layer))
             else:
 
                 @pl.when(outer < z.owners)
@@ -367,12 +400,12 @@
                     grads.at[layer, mats, share_rows(sec)],
                     {"section": lax.rem(sec + step, S)},
                 )
-            stage_sent(layer, first, stage, lambda: v.from_section.at[layer, :, mats], 1)
+            stage_sent(layer, first, stage, lambda: v.from_section.at[layer, :, mats], owner(layer))
         elif stage == CORE_BACK:
             stage_copy(
                 layer, first, stage, grads.at[layer, mats], grads.at[layer, mats], {"nodes": mate}
             )
-            stage_sent(layer, first, stage, lambda: grads.at[layer, mats], 1)
+            stage_sent(layer, first, stage, lambda: grads.at[layer, mats], owner(layer))
 
     def end_stage(stage, layer, first, count):
         mats = pl.ds(first, count)
@@ -388,6 +421,12 @@
                 for step in range(S - 1):
                     value = value + v.from_section[layer, step, mat]
                 v.sums[layer, mat, share_rows(sec), :] = value
+        elif stage == OUTER and layer in SHARED:
+            wait_bytes(v.shares.at[first, pl.ds(1, O - 1)], taken)
+            value = v.shares[first, 0]
+            for other in range(1, O):
+                value = value + v.shares[first, other]
+            grads[layer, first, share_rows(sec), :] = value
         elif stage == OUTER:
 
             def add():
@@ -417,17 +456,16 @@
         elif stage == CORE_BACK:
             wait_bytes(grads.at[layer, mats], taken)
 
-    def advance(*moves):
+    def stage_after(stage, layer):
+        return SECTION_BACK if stage == OUTER and layer in SHARED else stage + 1
+
+    def advance(layer, *moves):
         def run():
-            for stage, layer, first, count in moves:
-                if stage == CORE:
-                    for mat in range(first, first + count):
-                        end_stage(CORE, layer, mat, 1)
-                else:
-                    end_stage(stage, layer, first, count)
-                start_stage(stage + 1, layer, first, count)
-
-        on(1, run)
+            for stage, mat in moves:
+                end_stage(stage, layer, mat, 1)
+                start_stage(stage_after(stage, layer), layer, mat, 1)
+
+        on(owner(layer), run)
 
 
     loads[1].wait()
@@ -482,12 +520,13 @@
     v.prep_t[...] = v.prep[...].T
     for slot in range(1, K):
         column = v.prep_t[:, slot : slot + 1]
-        v.pick[slot - 1] = as_ones(iota((R, T), 1).astype(F32) == column)
+        pick = as_ones(iota((R, T), 1).astype(F32) == column)
+        v.pick[slot - 1, :, pl.ds(0, T)] = pick
+        v.pick[slot - 1, :, pl.ds(T, z.halo_pad)] = pick[:, R:]
         row = v.prep[slot : slot + 1, :]
         v.pick_t[:, (slot - 1) * R : slot * R] = as_ones(iota((z.picked, R), 0).astype(F32) == row)
-    group = D // HEADS
-    block_row = lax.div(lax.rem(iota((2 * D, D), 0), D), group)
-    v.ones[...] = as_ones(block_row == lax.div(iota((2 * D, D), 1), group))
+    block_row = lax.div(lax.rem(iota((2 * D, D), 0), D), GROUP)
+    v.ones[...] = as_ones(block_row == lax.div(iota((2 * D, D), 1), GROUP))
 
     def project(layer):
         rows = pl.ds(0, R)
@@ -504,8 +543,8 @@
         rows = pl.ds(R, z.halo_pad)
         left = mm3((v.h_hi[rows, :], v.h_lo[rows, :]), weight(layer, 0))
         high, low = halves(left)
-        v.table_hi[rows, :] = high
-        v.table_lo[rows, :] = low
+        v.halo_table[pl.ds(0, z.halo_pad), :] = high
+        v.halo_table[pl.ds(z.halo_pad, z.halo_pad), :] = low
 
     def store_halo(values):
         if z.halo < z.halo_pad:
@@ -536,13 +575,34 @@
         v.pair[slot, rows, pl.ds(0, D)] = high
         v.pair[slot, rows, pl.ds(D, D)] = low
 
-    def attend(layer):
-        def gather(slot, carry):
-            pick = v.pick[slot - 1]
+    def gather_own(layer):
+        def one(slot, carry):
+            pick = v.pick[slot - 1, :, pl.ds(0, R)]
             v.taken[layer, slot] = mm(pick, v.table_hi[...]) + mm(pick, v.table_lo[...])
             return carry
 
-        lax.fori_loop(1, K, gather, 0, unroll=True)
+        lax.fori_loop(1, K, one, 0, unroll=True)
+
+    def gather_halo(layer):
+        def one(slot, carry):
+            pick = v.pick[slot - 1, :, pl.ds(R, 2 * z.halo_pad)]
+            v.taken[layer, slot] = v.taken[layer, slot] + mm(pick, v.halo_table[...])
+            return carry
+
+        lax.fori_loop(1, K, one, 0, unroll=True)
+
+    def gather_all(layer):
+        def one(slot, carry):
+            own = v.pick[slot - 1, :, pl.ds(0, R)]
+            halo = v.pick[slot - 1, :, pl.ds(R, 2 * z.halo_pad)]
+            v.taken[layer, slot] = (
+                mm(own, v.table_hi[...]) + mm(own, v.table_lo[...]) + mm(halo, v.halo_table[...])
+            )
+            return carry
+
+        lax.fori_loop(1, K, one, 0, unroll=True)
+
+    def attend(layer):
         vector = v.vector_in[layer : layer + 1, :]
 
         def activate(i, carry):
@@ -550,9 +610,7 @@
             right = v.right[layer, rows, :]
             for slot in range(K):
                 u = v.taken[layer, slot, rows, :] + right
-                sig = 1.0 / (1.0 + jnp.exp(-u))
-                v.sig[layer, slot, rows, :] = sig
-                store_pair(slot, rows, u * sig * vector)
+                store_pair(slot, rows, u * sigmoid(u) * vector)
             return carry
 
         rows_loop(activate, 0)
@@ -581,6 +639,22 @@
         first, second = rows_loop(mix, (nothing, nothing))
         return add_rows(first), add_rows(second)
 
+    def derive(layer):
+        vector = v.vector_in[layer : layer + 1, :]
+
+        def one(i, carry):
+            rows = chunk(i)
+            right = v.right[layer, rows, :]
+            for slot in range(K):
+                u = v.taken[layer, slot, rows, :] + right
+                sig = sigmoid(u)
+                act = u * sig
+                v.act[layer, slot, rows, :] = act
+                v.rise[layer, slot, rows, :] = vector * (sig + act * (1.0 - sig))
+            return carry
+
+        rows_loop(one, 0)
+
     def moments(which):
         first, second = arrived_sums(which)
         mean = first / total_rows
@@ -600,13 +674,16 @@
         return mm(v.list[...], high) + mm(v.list[...], low)
 
     project(0)
+    gather_own(0)
     end_exchange(FEATURES)
     store_halo(arrived_rows(FEATURES))
     project_halo(0)
+    gather_halo(0)
     first, second = attend(0)
     v.outgoing[MIXED] = with_sums(list_rows(v.mixed[...]), first, second)
     start_exchange(MIXED)
     keep_transposed(0)
+    derive(0)
     end_exchange(MIXED)
     mean0, inverse0 = moments(MIXED)
 
@@ -629,10 +706,12 @@
 
     project(1)
     project_halo(1)
+    gather_all(1)
     first, second = attend(1)
     sums_tile(SUMS, first, second)
     start_exchange(SUMS, True)
     keep_transposed(1)
+    derive(1)
     loads[11].wait()
     end_exchange(SUMS)
     mean1, inverse1 = moments(SUMS)
@@ -670,8 +749,6 @@
         rows_loop(one, 0)
 
     def attend_back(layer, between=None):
-        vector = v.vector_in[layer : layer + 1, :]
-
         def differences(i, carry):
             rows = chunk(i)
             joined = v.joined[layer, rows, :]
@@ -685,16 +762,13 @@
 
         def one(i, carry):
             rows = chunk(i)
-            right = v.right[layer, rows, :]
             dmixed = v.dmixed[rows, :]
             dright = jnp.zeros((CHUNK, D), F32)
             for slot in range(K):
-                u = v.taken[layer, slot, rows, :] + right
-                sig = v.sig[layer, slot, rows, :]
                 alpha = v.alpha[layer, slot, rows, :]
                 dscore = alpha * v.score[slot, rows, :]
-                carry = carry + fold(dscore * u * sig)
-                du = dscore * vector * sig * (1.0 + u * (1.0 - sig))
+                carry = carry + fold(dscore * v.act[layer, slot, rows, :])
+                du = dscore * v.rise[layer, slot, rows, :]
                 dright = dright + du
                 dleft = du + alpha * dmixed
                 if slot == 0:
@@ -717,18 +791,39 @@
             pick = v.pick_t[rows, :]
             return mm(pick, v.dleft_hi[...]) + mm(pick, v.dleft_lo[...])
 
-        def scatter():
-            rows = pl.ds(0, R)
-            high, low = halves(scattered(rows) + v.dleft_self[...])
-            v.dl_hi[rows, :] = high
-            v.dl_lo[rows, :] = low
-            rows = pl.ds(R, z.halo)
-            high, low = halves(scattered(rows))
-            v.dl_hi[rows, :] = high
-            v.dl_lo[rows, :] = low
-
-        scatter()
+        rows = pl.ds(0, R)
+        own = scattered(rows) + v.dleft_self[...]
+        v.dleft_self[...] = own
+        high, low = halves(own)
+        v.dl_hi[rows, :] = high
+        v.dl_lo[rows, :] = low
+        rows = pl.ds(R, z.halo)
+        halo = scattered(rows)
+        if layer == 0:
+            start_return(halo)
+        high, low = halves(halo)
+        v.dl_hi[rows, :] = high
+        v.dl_lo[rows, :] = low
         return add_rows(vector_sum)
+
+    def start_return(halo):
+        v.returning[...] = halo[:, :LANES] + pltpu.roll(halo[:, LANES:], z.send, 0)
+        own = pl.ds(pl.multiple_of(me * TILE, TILE), TILE)
+
+        def send(step, carry):
+            other = lax.rem(me + step, N)
+            pltpu.make_async_remote_copy(
+                src_ref=v.returning.at[pl.ds(pl.multiple_of(other * TILE, TILE), TILE)],
+                dst_ref=v.returned.at[own],
+                send_sem=v.give_rows.at[0],
+                recv_sem=v.take_rows.at[0],
+                device_id={"nodes": other},
+                device_id_type=MESH,
+            ).start()
+            return carry
+
+        lax.fori_loop(1, N, send, 0)
+        v.returned[own, :] = v.returning[own, :]
 
     def dleft(rows):
         return v.dl_hi[rows, :], v.dl_lo[rows, :]
@@ -769,68 +864,170 @@
     start_exchange(BACK_ROWS)
     for mat in (2, 1, 0):
         weight_grad(1, mat)
-    advance((CORE, 1, 0, 3))
+    advance(1, (CORE, 2), (CORE, 1), (CORE, 0))
     end_exchange(BACK_ROWS)
     v.dpre[...] = (v.dh[...] + give_rows_back(BACK_ROWS)) * v.slope[0]
 
     normalization_back(0, BACK_ROWS, inverse0)
     weight_grad(0, 2)
-    vector0 = attend_back(0, lambda: weight_grad(0, 1))
+
+    def between():
+        weight_grad(0, 1)
+        advance(1, (SECTION, 2))
+        advance(0, (CORE, 2))
+
+    vector0 = attend_back(0, between)
     weight_grad(0, 0)
 
     row = iota((TILE, D), 0)
     tile = jnp.zeros((TILE, D), F32)
     for place, value in enumerate((vector0, vector1, gain0, gain1, shift0, shift1)):
         tile = jnp.where(row == place, value, tile)
-    v.outgoing[SMALL, pl.ds(0, TILE), :] = tile
-    start_exchange(SMALL, True)
-    advance((CORE, 0, 1, 2))
-    halo_back = input_back(0)
-    v.outgoing[INPUT_ROWS] = halo_back
-    start_exchange(INPUT_ROWS)
-    advance((SECTION, 1, 0, 3), (CORE, 0, 0, 1), (SECTION, 0, 1, 2))
-    end_exchange(SMALL)
-    v.small[...] = jnp.sum(v.incoming[SMALL].reshape(N, TILE, D), axis=0)
-    for step in range(1, S):
+    v.small[0] = tile
+
+    def send_small(stage, source, target, device):
         pltpu.make_async_remote_copy(
-            src_ref=v.small,
-            dst_ref=v.small_in.at[step],
-            send_sem=v.give_small.at[0],
-            recv_sem=v.take_small.at[0],
-            device_id={"section": lax.rem(sec + step, S)},
+            src_ref=source,
+            dst_ref=target,
+            send_sem=v.give_small.at[stage],
+            recv_sem=v.take_small.at[stage],
+            device_id=device,
             device_id_type=MESH,
         ).start()
-    advance((OUTER, 1, 0, 3), (SECTION, 0, 0, 1), (OUTER, 0, 1, 2))
-    end_exchange(INPUT_ROWS)
-    grad_in[0] = v.dh[...] + give_rows_back(INPUT_ROWS)
-    advance((OUTER_BACK, 1, 0, 3), (OUTER, 0, 0, 1), (OUTER_BACK, 0, 1, 2))
-    wait_bytes(v.small_in.at[pl.ds(1, S - 1)], v.take_small.at[0])
-    value = v.small[...]
-    for step in range(1, S):
-        value = value + v.small_in[step]
-    g_vec[...] = value[0:2, :]
-    g_gain[...] = value[2:4, :]
-    g_shift[...] = value[4:6, :]
-    advance((SECTION_BACK, 1, 0, 3), (OUTER_BACK, 0, 0, 1), (SECTION_BACK, 0, 1, 2))
-    advance((SECTION_BACK, 0, 0, 1))
-
-    def receive():
-        end_stage(CORE_BACK, 1, 0, 3)
-        end_stage(CORE_BACK, 0, 1, 2)
-        end_stage(CORE_BACK, 0, 0, 1)
-
-    on(0, receive)
+
+    on(0, lambda: send_small(0, v.small.at[0], v.small_core.at[0], {"nodes": mate}))
+
+    def small_outer():
+        wait_bytes(v.small_core.at[0], v.take_small.at[0])
+        value = v.small[0] + v.small_core[0]
+        v.small[1] = value
+        v.small_outer[outer] = value
+        for step in range(1, O):
+            send_small(
+                1, v.small.at[1], v.small_outer.at[outer], outer_device(lax.rem(outer + step, O))
+            )
+
+    def small_section():
+        wait_bytes(v.small_outer.at[pl.ds(1, O - 1)], v.take_small.at[1])
+        value = jnp.sum(v.small_outer[...], axis=0)
+        v.small[2] = value
+        v.small_section[sec] = value
+        for step in range(1, S):
+            send_small(
+                2, v.small.at[2], v.small_section.at[sec], {"section": lax.rem(sec + step, S)}
+            )
+
+    def put_small(value):
+        g_vec[...] = value[0:2, :]
+        g_gain[...] = value[2:4, :]
+        g_shift[...] = value[4:6, :]
+
+    def small_back():
+        wait_bytes(v.small_section.at[pl.ds(1, S - 1)], v.take_small.at[2])
+        value = jnp.sum(v.small_section[...], axis=0)
+        v.small[3] = value
+        send_small(3, v.small.at[3], v.small_core.at[1], {"nodes": mate})
+        put_small(value)
+
+    def small_end():
+        wait_bytes(v.small_core.at[1], v.take_small.at[3])
+        put_small(v.small_core[1])
+
+    advance(1, (SECTION, 1))
+    advance(0, (CORE, 1))
+    def part_input():
+        v.dh[...] = mm3((v.dr_hi[...], v.dr_lo[...]), weight(0, 1), mm_nt) + mm3(
+            (v.dm_hi[...], v.dm_lo[...]), weight(0, 2), mm_nt
+        )
+
+    def store_input():
+        wait_bytes(v.returned.at[pl.ds(0, (N - 1) * TILE)], v.take_rows.at[0])
+        values = v.returned[...]
+        values = jnp.concatenate([values, pltpu.roll(values, z.halo - z.send, 0)], axis=1)
+        high, low = halves(jnp.where(row_in_tile(z.halo) < z.send, values, 0.0))
+        listed = v.list_t[:, : z.halo]
+        left = v.dleft_self[...] + (mm(listed, high) + mm(listed, low))
+        grad_in[0] = v.dh[...] + mm3(halves(left), weight(0, 0), mm_nt)
+
+    tails = {
+        1: (
+            (SECTION, 0),
+            (OUTER, 2),
+            part_input,
+            (OUTER, 1),
+            (OUTER, 0),
+            store_input,
+            (OUTER_BACK, 2),
+            (OUTER_BACK, 1),
+            (OUTER_BACK, 0),
+            (SECTION_BACK, 2),
+            (SECTION_BACK, 1),
+            (SECTION_BACK, 0),
+            small_end,
+        ),
+        0: (
+            (CORE, 0),
+            (SECTION, 2),
+            small_outer,
+            (SECTION, 1),
+            (SECTION, 0),
+            part_input,
+            (OUTER, 2),
+            (OUTER, 1),
+            (OUTER, 0),
+            store_input,
+            small_section,
+            (OUTER_BACK, 2),
+            (OUTER_BACK, 1),
+            (OUTER_BACK, 0),
+            small_back,
+            (SECTION_BACK, 2),
+            (SECTION_BACK, 1),
+            (SECTION_BACK, 0),
+        ),
+    }
+
+    def finish(layer):
+        for step in tails[layer]:
+            if callable(step):
+                step()
+            else:
+                end_stage(step[0], layer, step[1], 1)
+                start_stage(stage_after(step[0], layer), layer, step[1], 1)
+
+    on(owner(1), lambda: finish(1))
+    on(owner(0), lambda: finish(0))
+
+    def receive(layer):
+        for mat in range(3):
+            end_stage(CORE_BACK, layer, mat, 1)
+
+    on(0, lambda: receive(0))
+    on(1, lambda: receive(1))
     for which in range(EXCHANGES):
         wait_bytes(v.outgoing.at[which, pl.ds(0, (N - 1) * TILE)], v.give.at[which])
-    wait_bytes(v.small_in.at[pl.ds(1, S - 1)], v.give_small.at[0])
+    wait_bytes(v.returned.at[pl.ds(0, (N - 1) * TILE)], v.give_rows.at[0])
 
     def sent(which):
         for ref, semaphore, sender in sends_to_end:
             if sender == which:
                 wait_bytes(ref(), semaphore())
 
-    on(0, lambda: sent(0))
-    on(1, lambda: sent(1))
+    def sent_small(stage, count):
+        wait_bytes(v.small_outer.at[pl.ds(0, count)], v.give_small.at[stage])
+
+    def sent0():
+        sent(0)
+        sent_small(0, 1)
+
+    def sent1():
+        sent(1)
+        sent_small(1, O - 1)
+        wait_bytes(v.small_section.at[pl.ds(1, S - 1)], v.give_small.at[2])
+        sent_small(3, 1)
+
+    on(0, sent0)
+    on(1, sent1)
 
 
 def store_kernel(*refs):
@@ -862,7 +1059,7 @@
 ):
     batches, rows, width = features.shape
     sections = lax.axis_size("section")
-    assert batches == sections
+    assert batches == sections and width == HEADS * GROUP
     z = sizes_of(
         sections, lax.axis_size("nodes"), rows, width, neighbours.shape[2], send_rows.shape[1]
     )

time: 68.7 us -> 63 us (0.917)
  Pallas kernels: 67.9 us -> 62.2 us
    pallas_call x1, Pallas kernels: 66.5 us -> 60.7 us  [body(): pl.pallas_call(functools.partial(kernel, z, names), out_shape=tuple((pltp...]
where the time goes in v4:
time: 63 us; the launch traced here: 62.8 us
  Pallas kernels  62.2 us (99%)
  between operations  0.65 us (1%)
    pallas_call x1, Pallas kernels, body(): pl.pallas_call(functools.partial(kernel, z, names), out_shape=tuple((pltp...  60.7 us
    pallas_call x1, Pallas kernels, body(): pl.pallas_call(store_kernel, out_shape=results, in_specs=[anywhere] * 6,...  1.41 us

profile of v4, /device:TPU:0, one launch (start us, length us, event | category | flops | bytes accessed | tf_op | source)
XLA Modules:
  0.0 62.8 jit_solution(16259588558878835338)
XLA Ops:
  0.6 60.7 %shard_map.179 = (f32[1,256,256]{2,1,0:T(8,128)S(1)}, f32[1,256,256]{2,1,0:T(8,128)S(1)}, f32[2,3,256,256]{3,2,1,0:T(8,128)S(1)}, f32[2,256]{1,0:T(2,128)S(1)}, ...) custom-call(f32[4,256,256]{2,1,0:T(8,128)} %refs_0_.1, f32[4,256,256]{2,1,0:T(8,128)} %refs_1_.1, s32[4,256]{1,0:T(4,128)} %refs_2_.1, ...), custom_call_target="tpu_custom_call" | custom-call | tf_op jit(solution)/shard_map/pallas_call | solution.py:1081
  61.4 1.4 %shard_map.180 = (f32[1,256,256]{2,1,0:T(8,128)}, f32[1,256,256]{2,1,0:T(8,128)}, f32[2,256,256]{2,1,0:T(8,128)}, f32[2,256,256]{2,1,0:T(8,128)}, f32[2,256,256]...) custom-call(f32[1,256,256]{2,1,0:T(8,128)S(1)} %get-tuple-element.14.refs_0_, ...), custom_call_target="tpu_custom_call" | custom-call | tf_op jit(solution)/shard_map/pallas_call | solution.py:1104

commit v5 on v4

--- a/solution.py
+++ b/solution.py
@@ -14,8 +14,9 @@
 F32 = jnp.float32
 BF16 = jnp.bfloat16
 MESH = pl.DeviceIdType.MESH
-UNROLL = 4
-SHARED = ()
+UNROLL = 16
+BLOCK = 32
+OUTER_FIRST = ()
 LANES = 128
 GROUP = 64
 TILE = 8
@@ -23,7 +24,7 @@
 
 FEATURES, MIXED, SUMS, BACK_SUMS, BACK_ROWS = range(5)
 EXCHANGES = 5
-CORE, SECTION, OUTER, OUTER_BACK, SECTION_BACK, CORE_BACK = range(6)
+CORE, FIRST, SECOND, SECOND_BACK, FIRST_BACK, CORE_BACK = range(6)
 STAGES = 6
 
 
@@ -65,10 +66,13 @@
     z.halo_pad = -(-z.halo // LANES) * LANES
     z.table = rows + z.halo_pad
     z.picked = rows + z.halo
-    z.share = rows // sections
-    z.piece = max(TILE, z.share // z.outer)
-    z.owners = z.share // z.piece
     return z
+
+
+def shares_of(rows, first, second):
+    share = rows // first
+    piece = max(TILE, share // second)
+    return share, piece, share // piece
 
 
 def scratch_of(z):
@@ -139,10 +143,13 @@
         "returned": ((z.halo, LANES), F32),
         "sums": ((2, 3, R, D), F32),
         "from_core": ((2, 3, R, D), F32),
-        "from_section": ((2, S - 1, 3, z.share, D), F32),
-        "from_outer": ((2, O, 3, z.piece, D), F32),
-        "shares": ((3, O, z.share, D), F32),
     }
+    for layer in range(2):
+        for mat in range(3):
+            first, second = (O, S) if (layer, mat) in OUTER_FIRST else (S, O)
+            share, piece, _ = shares_of(R, first, second)
+            vmem[f"first_{layer}{mat}"] = ((first - 1, share, D), F32)
+            vmem[f"second_{layer}{mat}"] = ((second, piece, D), F32)
     return vmem
 
 
@@ -288,17 +295,22 @@
     def stage_sent(layer, first, stage, ref, which):
         sends_to_end.append((ref, lambda: v.give_stage.at[layer, first, stage], which))
 
-    def share_rows(which):
-        return pl.ds(pl.multiple_of(which * z.share, TILE), z.share)
-
-    def piece_rows(which):
-        return pl.ds(pl.multiple_of(sec * z.share + which * z.piece, TILE), z.piece)
-
-    def outer_device(which):
-        return {"nodes": which * 2 + core}
-
-    def from_others(layer, mats, count):
-        return v.from_outer.at[layer, pl.ds(1, count), mats]
+    def lane_of(layer, mat):
+        lane = types.SimpleNamespace()
+        over_section = (S, sec, lambda which: {"section": which})
+        over_outer = (O, outer, lambda which: {"nodes": which * 2 + core})
+        axes = (over_outer, over_section) if (layer, mat) in OUTER_FIRST else (over_section, over_outer)
+        (lane.first, lane.first_me, lane.first_device), (lane.second, lane.second_me, lane.second_device) = axes
+        lane.share, lane.piece, lane.owners = shares_of(R, lane.first, lane.second)
+        lane.sums = v.sums.at[layer, mat]
+        lane.result = grads.at[layer, mat]
+        lane.from_first = getattr(v, f"first_{layer}{mat}")
+        lane.from_second = getattr(v, f"second_{layer}{mat}")
+        lane.share_rows = lambda which: pl.ds(pl.multiple_of(which * lane.share, TILE), lane.share)
+        lane.piece_rows = lambda which: pl.ds(
+            pl.multiple_of(lane.first_me * lane.share + which * lane.piece, TILE), lane.piece
+        )
+        return lane
 
     def start_core(layer, mat):
         on(
@@ -309,161 +321,131 @@
         )
         stage_sent(layer, mat, CORE, lambda: v.from_core.at[layer, mat], 1 - owner(layer))
 
-    def start_stage(stage, layer, first, count):
-        mats = pl.ds(first, count)
-        if stage == SECTION:
-            for step in range(1, S):
-                other = lax.rem(sec + step, S)
-                stage_copy(
-                    layer,
-                    first,
-                    stage,
-                    v.sums.at[layer, mats, share_rows(other)],
-                    v.from_section.at[layer, step - 1, mats],
-                    {"section": other},
+    def start_stage(stage, layer, mat):
+        lane = lane_of(layer, mat)
+        copy = functools.partial(stage_copy, layer, mat, stage)
+
+        def sent(ref):
+            stage_sent(layer, mat, stage, ref, owner(layer))
+
+        if stage == FIRST:
+            for step in range(1, lane.first):
+                other = lax.rem(lane.first_me + step, lane.first)
+                copy(
+                    lane.sums.at[lane.share_rows(other)],
+                    lane.from_first.at[step - 1],
+                    lane.first_device(other),
                 )
-            stage_sent(layer, first, stage, lambda: v.from_section.at[layer, :, mats], owner(layer))
-        elif stage == OUTER and layer in SHARED:
-            for step in range(1, O):
-                stage_copy(
-                    layer,
-                    first,
-                    stage,
-                    v.sums.at[layer, first, share_rows(sec)],
-                    v.shares.at[first, outer],
-                    outer_device(lax.rem(outer + step, O)),
-                )
-            stage_sent(layer, first, stage, lambda: v.shares.at[first, pl.ds(1, O - 1)], owner(layer))
-            v.shares[first, outer] = v.sums[layer, first, share_rows(sec), :]
-        elif stage == OUTER:
-            if z.owners == O:
-                for step in range(1, O):
-                    other = lax.rem(outer + step, O)
-                    stage_copy(
-                        layer,
-                        first,
-                        stage,
-                        v.sums.at[layer, mats, piece_rows(other)],
-                        v.from_outer.at[layer, step, mats],
-                        outer_device(other),
+            sent(lambda: lane_of(layer, mat).from_first)
+        elif stage == SECOND:
+            if lane.owners == lane.second:
+                for step in range(1, lane.second):
+                    other = lax.rem(lane.second_me + step, lane.second)
+                    copy(
+                        lane.sums.at[lane.piece_rows(other)],
+                        lane.from_second.at[step],
+                        lane.second_device(other),
                     )
-                stage_sent(layer, first, stage, lambda: from_others(layer, mats, O - 1), owner(layer))
+                sent(lambda: lane_of(layer, mat).from_second.at[pl.ds(1, lane.second - 1)])
             else:
-                for other in range(z.owners):
-
-                    @pl.when(outer != other)
+                for other in range(lane.owners):
+
+                    @pl.when(lane.second_me != other)
                     def _():
-                        stage_copy(
-                            layer,
-                            first,
-                            stage,
-                            v.sums.at[layer, mats, piece_rows(other)],
-                            v.from_outer.at[layer, lax.rem(outer - other + O, O), mats],
-                            outer_device(other),
+                        copy(
+                            lane.sums.at[lane.piece_rows(other)],
+                            lane.from_second.at[
+                                lax.rem(lane.second_me - other + lane.second, lane.second)
+                            ],
+                            lane.second_device(other),
                         )
-                        wait_bytes(
-                            v.from_outer.at[layer, 0, mats], v.give_stage.at[layer, first, stage]
-                        )
-
-        elif stage == OUTER_BACK:
+                        wait_bytes(lane.from_second.at[0], v.give_stage.at[layer, mat, stage])
+
+        elif stage == SECOND_BACK:
 
             def send_all():
-                for step in range(1, O):
-                    stage_copy(
-                        layer,
-                        first,
-                        stage,
-                        grads.at[layer, mats, piece_rows(outer)],
-                        grads.at[layer, mats, piece_rows(outer)],
-                        outer_device(lax.rem(outer + step, O)),
+                rows = lane.piece_rows(lane.second_me)
+                for step in range(1, lane.second):
+                    copy(
+                        lane.result.at[rows],
+                        lane.result.at[rows],
+                        lane.second_device(lax.rem(lane.second_me + step, lane.second)),
                     )
 
-            if z.owners == O:
+            if lane.owners == lane.second:
                 send_all()
-                stage_sent(layer, first, stage, lambda: from_others(layer, mats, O - 1), owner(layer))
+                sent(lambda: lane_of(layer, mat).from_second.at[pl.ds(1, lane.second - 1)])
             else:
 
-                @pl.when(outer < z.owners)
+                @pl.when(lane.second_me < lane.owners)
                 def _():
                     send_all()
                     wait_bytes(
-                        from_others(layer, mats, O - 1), v.give_stage.at[layer, first, stage]
+                        lane.from_second.at[pl.ds(1, lane.second - 1)],
+                        v.give_stage.at[layer, mat, stage],
                     )
 
-        elif stage == SECTION_BACK:
-            for step in range(1, S):
-                stage_copy(
-                    layer,
-                    first,
-                    stage,
-                    grads.at[layer, mats, share_rows(sec)],
-                    grads.at[layer, mats, share_rows(sec)],
-                    {"section": lax.rem(sec + step, S)},
+        elif stage == FIRST_BACK:
+            rows = lane.share_rows(lane.first_me)
+            for step in range(1, lane.first):
+                copy(
+                    lane.result.at[rows],
+                    lane.result.at[rows],
+                    lane.first_device(lax.rem(lane.first_me + step, lane.first)),
                 )
-            stage_sent(layer, first, stage, lambda: v.from_section.at[layer, :, mats], owner(layer))
+            sent(lambda: lane_of(layer, mat).from_first)
         elif stage == CORE_BACK:
-            stage_copy(
-                layer, first, stage, grads.at[layer, mats], grads.at[layer, mats], {"nodes": mate}
-            )
-            stage_sent(layer, first, stage, lambda: grads.at[layer, mats], owner(layer))
-
-    def end_stage(stage, layer, first, count):
-        mats = pl.ds(first, count)
-        taken = v.take_stage.at[layer, first, stage]
-        each = range(first, first + count)
+            copy(lane.result, lane.result, {"nodes": mate})
+            sent(lambda: grads.at[layer, mat])
+
+    def end_stage(stage, layer, mat):
+        lane = lane_of(layer, mat)
+        taken = v.take_stage.at[layer, mat, stage]
         if stage == CORE:
-            wait_bytes(v.from_core.at[layer, first], taken)
-            v.sums[layer, first] = v.sums[layer, first] + v.from_core[layer, first]
-        elif stage == SECTION:
-            wait_bytes(v.from_section.at[layer, :, mats], taken)
-            for mat in each:
-                value = v.sums[layer, mat, share_rows(sec), :]
-                for step in range(S - 1):
-                    value = value + v.from_section[layer, step, mat]
-                v.sums[layer, mat, share_rows(sec), :] = value
-        elif stage == OUTER and layer in SHARED:
-            wait_bytes(v.shares.at[first, pl.ds(1, O - 1)], taken)
-            value = v.shares[first, 0]
-            for other in range(1, O):
-                value = value + v.shares[first, other]
-            grads[layer, first, share_rows(sec), :] = value
-        elif stage == OUTER:
+            wait_bytes(v.from_core.at[layer, mat], taken)
+            v.sums[layer, mat] = v.sums[layer, mat] + v.from_core[layer, mat]
+        elif stage == FIRST:
+            wait_bytes(lane.from_first, taken)
+            rows = lane.share_rows(lane.first_me)
+            value = v.sums[layer, mat, rows, :]
+            for step in range(lane.first - 1):
+                value = value + lane.from_first[step]
+            v.sums[layer, mat, rows, :] = value
+        elif stage == SECOND:
 
             def add():
-                wait_bytes(from_others(layer, mats, O - 1), taken)
-                for mat in each:
-                    value = v.sums[layer, mat, piece_rows(outer), :]
-                    for step in range(1, O):
-                        value = value + v.from_outer[layer, step, mat]
-                    grads[layer, mat, piece_rows(outer), :] = value
-
-            if z.owners == O:
+                wait_bytes(lane.from_second.at[pl.ds(1, lane.second - 1)], taken)
+                rows = lane.piece_rows(lane.second_me)
+                value = v.sums[layer, mat, rows, :]
+                for step in range(1, lane.second):
+                    value = value + lane.from_second[step]
+                grads[layer, mat, rows, :] = value
+
+            if lane.owners == lane.second:
                 add()
             else:
-                pl.when(outer < z.owners)(add)
-        elif stage == OUTER_BACK:
-            if z.owners == O:
-                wait_bytes(from_others(layer, mats, O - 1), taken)
+                pl.when(lane.second_me < lane.owners)(add)
+        elif stage == SECOND_BACK:
+            if lane.owners == lane.second:
+                wait_bytes(lane.from_second.at[pl.ds(1, lane.second - 1)], taken)
             else:
-                wait_bytes(from_others(layer, mats, z.owners - 1), taken)
-
-                @pl.when(outer >= z.owners)
+                if lane.owners > 1:
+                    wait_bytes(lane.from_second.at[pl.ds(1, lane.owners - 1)], taken)
+
+                @pl.when(lane.second_me >= lane.owners)
                 def _():
-                    wait_bytes(v.from_outer.at[layer, 0, mats], taken)
-
-        elif stage == SECTION_BACK:
-            wait_bytes(v.from_section.at[layer, :, mats], taken)
+                    wait_bytes(lane.from_second.at[0], taken)
+
+        elif stage == FIRST_BACK:
+            wait_bytes(lane.from_first, taken)
         elif stage == CORE_BACK:
-            wait_bytes(grads.at[layer, mats], taken)
-
-    def stage_after(stage, layer):
-        return SECTION_BACK if stage == OUTER and layer in SHARED else stage + 1
+            wait_bytes(grads.at[layer, mat], taken)
 
     def advance(layer, *moves):
         def run():
             for stage, mat in moves:
-                end_stage(stage, layer, mat, 1)
-                start_stage(stage_after(stage, layer), layer, mat, 1)
+                end_stage(stage, layer, mat)
+                start_stage(stage + 1, layer, mat)
 
         on(owner(layer), run)
 
@@ -563,13 +545,6 @@
         v.ht_hi[layer] = high
         v.ht_lo[layer] = low
 
-    def head_sums():
-        def one(slot, carry):
-            v.score[slot] = mm(v.pair[slot], v.ones[...])
-            return carry
-
-        lax.fori_loop(0, K, one, 0, unroll=True)
-
     def store_pair(slot, rows, values):
         high, low = halves(values)
         v.pair[slot, rows, pl.ds(0, D)] = high
@@ -583,38 +558,35 @@
 
         lax.fori_loop(1, K, one, 0, unroll=True)
 
-    def gather_halo(layer):
-        def one(slot, carry):
-            pick = v.pick[slot - 1, :, pl.ds(R, 2 * z.halo_pad)]
-            v.taken[layer, slot] = v.taken[layer, slot] + mm(pick, v.halo_table[...])
-            return carry
-
-        lax.fori_loop(1, K, one, 0, unroll=True)
-
-    def gather_all(layer):
-        def one(slot, carry):
-            own = v.pick[slot - 1, :, pl.ds(0, R)]
-            halo = v.pick[slot - 1, :, pl.ds(R, 2 * z.halo_pad)]
-            v.taken[layer, slot] = (
-                mm(own, v.table_hi[...]) + mm(own, v.table_lo[...]) + mm(halo, v.halo_table[...])
-            )
-            return carry
-
-        lax.fori_loop(1, K, one, 0, unroll=True)
+    def head_sum(slot):
+        v.score[slot] = mm(v.pair[slot], v.ones[...])
 
     def attend(layer):
         vector = v.vector_in[layer : layer + 1, :]
 
-        def activate(i, carry):
-            rows = chunk(i)
-            right = v.right[layer, rows, :]
-            for slot in range(K):
-                u = v.taken[layer, slot, rows, :] + right
+        def gather(slot):
+            pick = v.pick[slot - 1, :, pl.ds(R, 2 * z.halo_pad)]
+            value = mm(pick, v.halo_table[...])
+            if layer == 0:
+                value = v.taken[layer, slot] + value
+            else:
+                pick = v.pick[slot - 1, :, pl.ds(0, R)]
+                value = mm(pick, v.table_hi[...]) + mm(pick, v.table_lo[...]) + value
+            v.taken[layer, slot] = value
+
+        def activate(slot):
+            for place in range(0, R, BLOCK):
+                rows = pl.ds(place, BLOCK)
+                u = v.taken[layer, slot, rows, :] + v.right[layer, rows, :]
                 store_pair(slot, rows, u * sigmoid(u) * vector)
-            return carry
-
-        rows_loop(activate, 0)
-        head_sums()
+
+        for slot in range(1, K + 3):
+            if slot < K:
+                gather(slot)
+            if slot <= K:
+                activate(slot - 1)
+            if slot >= 3:
+                head_sum(slot - 3)
 
         def mix(i, carry):
             rows = chunk(i)
@@ -678,7 +650,6 @@
     end_exchange(FEATURES)
     store_halo(arrived_rows(FEATURES))
     project_halo(0)
-    gather_halo(0)
     first, second = attend(0)
     v.outgoing[MIXED] = with_sums(list_rows(v.mixed[...]), first, second)
     start_exchange(MIXED)
@@ -706,7 +677,6 @@
 
     project(1)
     project_halo(1)
-    gather_all(1)
     first, second = attend(1)
     sums_tile(SUMS, first, second)
     start_exchange(SUMS, True)
@@ -749,16 +719,17 @@
         rows_loop(one, 0)
 
     def attend_back(layer, between=None):
-        def differences(i, carry):
-            rows = chunk(i)
-            joined = v.joined[layer, rows, :]
-            dmixed = v.dmixed[rows, :]
-            for slot in range(K):
-                store_pair(slot, rows, (v.taken[layer, slot, rows, :] - joined) * dmixed)
-            return carry
-
-        rows_loop(differences, 0)
-        head_sums()
+        def differences(slot):
+            for place in range(0, R, BLOCK):
+                rows = pl.ds(place, BLOCK)
+                value = (v.taken[layer, slot, rows, :] - v.joined[layer, rows, :]) * v.dmixed[rows, :]
+                store_pair(slot, rows, value)
+
+        for slot in range(K + 1):
+            if slot < K:
+                differences(slot)
+            if slot >= 1:
+                head_sum(slot - 1)
 
         def one(i, carry):
             rows = chunk(i)
@@ -873,7 +844,7 @@
 
     def between():
         weight_grad(0, 1)
-        advance(1, (SECTION, 2))
+        advance(1, (FIRST, 2))
         advance(0, (CORE, 2))
 
     vector0 = attend_back(0, between)
@@ -904,7 +875,7 @@
         v.small_outer[outer] = value
         for step in range(1, O):
             send_small(
-                1, v.small.at[1], v.small_outer.at[outer], outer_device(lax.rem(outer + step, O))
+                1, v.small.at[1], v.small_outer.at[outer], {"nodes": lax.rem(outer + step, O) * 2 + core}
             )
 
     def small_section():
@@ -933,7 +904,7 @@
         wait_bytes(v.small_core.at[1], v.take_small.at[3])
         put_small(v.small_core[1])
 
-    advance(1, (SECTION, 1))
+    advance(1, (FIRST, 1))
     advance(0, (CORE, 1))
     def part_input():
         v.dh[...] = mm3((v.dr_hi[...], v.dr_lo[...]), weight(0, 1), mm_nt) + mm3(
@@ -951,39 +922,39 @@
 
     tails = {
         1: (
-            (SECTION, 0),
-            (OUTER, 2),
+            (FIRST, 0),
+            (SECOND, 2),
             part_input,
-            (OUTER, 1),
-            (OUTER, 0),
+            (SECOND, 1),
+            (SECOND, 0),
             store_input,
-            (OUTER_BACK, 2),
-            (OUTER_BACK, 1),
-            (OUTER_BACK, 0),
-            (SECTION_BACK, 2),
-            (SECTION_BACK, 1),
-            (SECTION_BACK, 0),
+            (SECOND_BACK, 2),
+            (SECOND_BACK, 1),
+            (SECOND_BACK, 0),
+            (FIRST_BACK, 2),
+            (FIRST_BACK, 1),
+            (FIRST_BACK, 0),
             small_end,
         ),
         0: (
             (CORE, 0),
-            (SECTION, 2),
+            (FIRST, 2),
             small_outer,
-            (SECTION, 1),
-            (SECTION, 0),
+            (FIRST, 1),
+            (FIRST, 0),
             part_input,
-            (OUTER, 2),
-            (OUTER, 1),
-            (OUTER, 0),
+            (SECOND, 2),
+            (SECOND, 1),
+            (SECOND, 0),
             store_input,
             small_section,
-            (OUTER_BACK, 2),
-            (OUTER_BACK, 1),
-            (OUTER_BACK, 0),
+            (SECOND_BACK, 2),
+            (SECOND_BACK, 1),
+            (SECOND_BACK, 0),
             small_back,
-            (SECTION_BACK, 2),
-            (SECTION_BACK, 1),
-            (SECTION_BACK, 0),
+            (FIRST_BACK, 2),
+            (FIRST_BACK, 1),
+            (FIRST_BACK, 0),
         ),
     }
 
@@ -992,15 +963,15 @@
             if callable(step):
                 step()
             else:
-                end_stage(step[0], layer, step[1], 1)
-                start_stage(stage_after(step[0], layer), layer, step[1], 1)
+                end_stage(step[0], layer, step[1])
+                start_stage(step[0] + 1, layer, step[1])
 
     on(owner(1), lambda: finish(1))
     on(owner(0), lambda: finish(0))
 
     def receive(layer):
         for mat in range(3):
-            end_stage(CORE_BACK, layer, mat, 1)
+            end_stage(CORE_BACK, layer, mat)
 
     on(0, lambda: receive(0))
     on(1, lambda: receive(1))

time: 63 us -> 58.4 us (0.927)
  Pallas kernels: 62.2 us -> 57.4 us
    pallas_call x1, Pallas kernels: 60.7 us -> 56 us  [body(): pl.pallas_call(functools.partial(kernel, z, names), out_shape=tuple((pltp...]
where the time goes in v5:
time: 58.4 us; the launch traced here: 58.2 us
  Pallas kernels  57.4 us (98%)
  between operations  0.81 us (1%)
    pallas_call x1, Pallas kernels, body(): pl.pallas_call(functools.partial(kernel, z, names), out_shape=tuple((pltp...  56 us
    pallas_call x1, Pallas kernels, body(): pl.pallas_call(store_kernel, out_shape=results, in_specs=[anywhere] * 6,...  1.41 us

profile of v5, /device:TPU:0, one launch (start us, length us, event | category | flops | bytes accessed | tf_op | source)
XLA Modules:
  0.0 58.2 jit_solution(15149424050988913965)
XLA Ops:
  0.6 56.0 %shard_map.179 = (f32[1,256,256]{2,1,0:T(8,128)S(1)}, f32[1,256,256]{2,1,0:T(8,128)S(1)}, f32[2,3,256,256]{3,2,1,0:T(8,128)S(1)}, f32[2,256]{1,0:T(2,128)S(1)}, ...) custom-call(f32[4,256,256]{2,1,0:T(8,128)} %refs_0_.1, f32[4,256,256]{2,1,0:T(8,128)} %refs_1_.1, s32[4,256]{1,0:T(4,128)} %refs_2_.1, ...), custom_call_target="tpu_custom_call" | custom-call | tf_op jit(solution)/shard_map/pallas_call | solution.py:1052
  56.6 1.4 %shard_map.180 = (f32[1,256,256]{2,1,0:T(8,128)}, f32[1,256,256]{2,1,0:T(8,128)}, f32[2,256,256]{2,1,0:T(8,128)}, f32[2,256,256]{2,1,0:T(8,128)}, f32[2,256,256]...) custom-call(f32[1,256,256]{2,1,0:T(8,128)S(1)} %get-tuple-element.14.refs_0_, ...), custom_call_target="tpu_custom_call" | custom-call | tf_op jit(solution)/shard_map/pallas_call | solution.py:1075

commit v6 on v5

--- a/solution.py
+++ b/solution.py
@@ -26,6 +26,45 @@
 EXCHANGES = 5
 CORE, FIRST, SECOND, SECOND_BACK, FIRST_BACK, CORE_BACK = range(6)
 STAGES = 6
+ON_CORE_0 = ((1, 2), (1, 1))
+BETWEEN = ((FIRST, 1, 2), (FIRST, 1, 0), (CORE, 0, 2))
+AFTER = ((FIRST, 1, 1), (CORE, 0, 1))
+TAILS = (
+    (
+        (SECOND, 1, 2),
+        (SECOND, 1, 1),
+        (SECOND_BACK, 1, 2),
+        (SECOND_BACK, 1, 1),
+        (FIRST_BACK, 1, 2),
+        (FIRST_BACK, 1, 1),
+        "part",
+        "input",
+        "end",
+    ),
+    (
+        (CORE, 0, 0),
+        (SECOND, 1, 0),
+        (FIRST, 0, 2),
+        "outer",
+        (FIRST, 0, 1),
+        (FIRST, 0, 0),
+        (SECOND_BACK, 1, 0),
+        (SECOND, 0, 2),
+        (SECOND, 0, 1),
+        "section",
+        (SECOND, 0, 0),
+        (FIRST_BACK, 1, 0),
+        (SECOND_BACK, 0, 2),
+        (SECOND_BACK, 0, 1),
+        "back",
+        (SECOND_BACK, 0, 0),
+        (FIRST_BACK, 0, 2),
+        (FIRST_BACK, 0, 1),
+        (FIRST_BACK, 0, 0),
+        "part",
+        "input",
+    ),
+)
 
 
 def halves(values):
@@ -274,8 +313,8 @@
         listed = v.list_t[:, : z.halo]
         return mm(listed, high) + mm(listed, low)
 
-    def owner(layer):
-        return 1 - layer
+    def owner(layer, mat):
+        return 0 if (layer, mat) in ON_CORE_0 else 1
 
     sends_to_end = []
 
@@ -314,19 +353,19 @@
 
     def start_core(layer, mat):
         on(
-            1 - owner(layer),
+            1 - owner(layer, mat),
             lambda: stage_copy(
                 layer, mat, CORE, v.sums.at[layer, mat], v.from_core.at[layer, mat], {"nodes": mate}
             ),
         )
-        stage_sent(layer, mat, CORE, lambda: v.from_core.at[layer, mat], 1 - owner(layer))
+        stage_sent(layer, mat, CORE, lambda: v.from_core.at[layer, mat], 1 - owner(layer, mat))
 
     def start_stage(stage, layer, mat):
         lane = lane_of(layer, mat)
         copy = functools.partial(stage_copy, layer, mat, stage)
 
         def sent(ref):
-            stage_sent(layer, mat, stage, ref, owner(layer))
+            stage_sent(layer, mat, stage, ref, owner(layer, mat))
 
         if stage == FIRST:
             for step in range(1, lane.first):
@@ -441,13 +480,16 @@
         elif stage == CORE_BACK:
             wait_bytes(grads.at[layer, mat], taken)
 
-    def advance(layer, *moves):
-        def run():
-            for stage, mat in moves:
-                end_stage(stage, layer, mat)
-                start_stage(stage + 1, layer, mat)
-
-        on(owner(layer), run)
+    def advance(*moves):
+        def run(which):
+            for stage, layer, mat in moves:
+                if owner(layer, mat) == which:
+                    end_stage(stage, layer, mat)
+                    start_stage(stage + 1, layer, mat)
+
+        for which in range(2):
+            if any(owner(layer, mat) == which for _, layer, mat in moves):
+                on(which, functools.partial(run, which))
 
 
     loads[1].wait()
@@ -725,11 +767,13 @@
                 value = (v.taken[layer, slot, rows, :] - v.joined[layer, rows, :]) * v.dmixed[rows, :]
                 store_pair(slot, rows, value)
 
+        weight_grad(layer, 2)
         for slot in range(K + 1):
             if slot < K:
                 differences(slot)
             if slot >= 1:
                 head_sum(slot - 1)
+        start_core(layer, 2)
 
         def one(i, carry):
             rows = chunk(i)
@@ -816,7 +860,6 @@
             upstream = (v.dr_hi[...], v.dr_lo[...]) if mat == 1 else (v.dm_hi[...], v.dm_lo[...])
             inputs = (v.ht_hi[layer, :, pl.ds(0, R)], v.ht_lo[layer, :, pl.ds(0, R)])
         v.sums[layer, mat] = mm3(inputs, upstream)
-        start_core(layer, mat)
 
     if z.halo < z.halo_pad:
         rest = pl.ds(R + z.halo, z.halo_pad - z.halo)
@@ -833,22 +876,25 @@
     gain0 = add_rows(dpre * v.normed[0]) + add_rows(halo_dpre * v.halo_normed[...])
     v.outgoing[BACK_ROWS] = with_sums(halo_back, shift0, gain0)
     start_exchange(BACK_ROWS)
-    for mat in (2, 1, 0):
-        weight_grad(1, mat)
-    advance(1, (CORE, 2), (CORE, 1), (CORE, 0))
+    advance((CORE, 1, 2))
+    weight_grad(1, 1)
+    start_core(1, 1)
+    weight_grad(1, 0)
+    start_core(1, 0)
+    advance((CORE, 1, 1), (CORE, 1, 0))
     end_exchange(BACK_ROWS)
     v.dpre[...] = (v.dh[...] + give_rows_back(BACK_ROWS)) * v.slope[0]
 
     normalization_back(0, BACK_ROWS, inverse0)
-    weight_grad(0, 2)
 
     def between():
         weight_grad(0, 1)
-        advance(1, (FIRST, 2))
-        advance(0, (CORE, 2))
+        start_core(0, 1)
+        advance(*BETWEEN)
 
     vector0 = attend_back(0, between)
     weight_grad(0, 0)
+    start_core(0, 0)
 
     row = iota((TILE, D), 0)
     tile = jnp.zeros((TILE, D), F32)
@@ -904,8 +950,7 @@
         wait_bytes(v.small_core.at[1], v.take_small.at[3])
         put_small(v.small_core[1])
 
-    advance(1, (FIRST, 1))
-    advance(0, (CORE, 1))
+    advance(*AFTER)
     def part_input():
         v.dh[...] = mm3((v.dr_hi[...], v.dr_lo[...]), weight(0, 1), mm_nt) + mm3(
             (v.dm_hi[...], v.dm_lo[...]), weight(0, 2), mm_nt
@@ -920,61 +965,32 @@
         left = v.dleft_self[...] + (mm(listed, high) + mm(listed, low))
         grad_in[0] = v.dh[...] + mm3(halves(left), weight(0, 0), mm_nt)
 
-    tails = {
-        1: (
-            (FIRST, 0),
-            (SECOND, 2),
-            part_input,
-            (SECOND, 1),
-            (SECOND, 0),
-            store_input,
-            (SECOND_BACK, 2),
-            (SECOND_BACK, 1),
-            (SECOND_BACK, 0),
-            (FIRST_BACK, 2),
-            (FIRST_BACK, 1),
-            (FIRST_BACK, 0),
-            small_end,
-        ),
-        0: (
-            (CORE, 0),
-            (FIRST, 2),
-            small_outer,
-            (FIRST, 1),
-            (FIRST, 0),
-            part_input,
-            (SECOND, 2),
-            (SECOND, 1),
-            (SECOND, 0),
-            store_input,
-            small_section,
-            (SECOND_BACK, 2),
-            (SECOND_BACK, 1),
-            (SECOND_BACK, 0),
-            small_back,
-            (FIRST_BACK, 2),
-            (FIRST_BACK, 1),
-            (FIRST_BACK, 0),
-        ),
+    steps = {
+        "outer": small_outer,
+        "section": small_section,
+        "back": small_back,
+        "end": small_end,
+        "part": part_input,
+        "input": store_input,
     }
 
-    def finish(layer):
-        for step in tails[layer]:
-            if callable(step):
-                step()
+    def finish(which):
+        for step in TAILS[which]:
+            if isinstance(step, str):
+                steps[step]()
             else:
-                end_stage(step[0], layer, step[1])
-                start_stage(step[0] + 1, layer, step[1])
-
-    on(owner(1), lambda: finish(1))
-    on(owner(0), lambda: finish(0))
-
-    def receive(layer):
-        for mat in range(3):
-            end_stage(CORE_BACK, layer, mat)
-
-    on(0, lambda: receive(0))
-    on(1, lambda: receive(1))
+                end_stage(*step)
+                start_stage(step[0] + 1, *step[1:])
+
+    on(0, lambda: finish(0))
+    on(1, lambda: finish(1))
+
+    def receive(which):
+        for layer in (1, 0):
+            for mat in (2, 1, 0):
+                if owner(layer, mat) != which:
+                    end_stage(CORE_BACK, layer, mat)
+
     for which in range(EXCHANGES):
         wait_bytes(v.outgoing.at[which, pl.ds(0, (N - 1) * TILE)], v.give.at[which])
     wait_bytes(v.returned.at[pl.ds(0, (N - 1) * TILE)], v.give_rows.at[0])
@@ -990,12 +1006,14 @@
     def sent0():
         sent(0)
         sent_small(0, 1)
+        receive(0)
 
     def sent1():
         sent(1)
         sent_small(1, O - 1)
         wait_bytes(v.small_section.at[pl.ds(1, S - 1)], v.give_small.at[2])
         sent_small(3, 1)
+        receive(1)
 
     on(0, sent0)
     on(1, sent1)

time: 58.4 us -> 57.6 us (0.986)
  Pallas kernels: 57.4 us -> 56.6 us
    pallas_call x1, Pallas kernels: 56 us -> 55.2 us  [body(): pl.pallas_call(functools.partial(kernel, z, names), out_shape=tuple((pltp...]
where the time goes in v6:
time: 57.6 us; the launch traced here: 57.4 us
  Pallas kernels  56.6 us (98%)
  between operations  0.81 us (1%)
    pallas_call x1, Pallas kernels, body(): pl.pallas_call(functools.partial(kernel, z, names), out_shape=tuple((pltp...  55.2 us
    pallas_call x1, Pallas kernels, body(): pl.pallas_call(store_kernel, out_shape=results, in_specs=[anywhere] * 6,...  1.41 us

profile of v6, /device:TPU:0, one launch (start us, length us, event | category | flops | bytes accessed | tf_op | source)
XLA Modules:
  0.0 57.4 jit_solution(9046627002089012500)
XLA Ops:
  0.6 55.2 %shard_map.179 = (f32[1,256,256]{2,1,0:T(8,128)S(1)}, f32[1,256,256]{2,1,0:T(8,128)S(1)}, f32[2,3,256,256]{3,2,1,0:T(8,128)S(1)}, f32[2,256]{1,0:T(2,128)S(1)}, ...) custom-call(f32[4,256,256]{2,1,0:T(8,128)} %refs_0_.1, f32[4,256,256]{2,1,0:T(8,128)} %refs_1_.1, s32[4,256]{1,0:T(4,128)} %refs_2_.1, ...), custom_call_target="tpu_custom_call" | custom-call | tf_op jit(solution)/shard_map/pallas_call | solution.py:1070
  55.8 1.4 %shard_map.180 = (f32[1,256,256]{2,1,0:T(8,128)}, f32[1,256,256]{2,1,0:T(8,128)}, f32[2,256,256]{2,1,0:T(8,128)}, f32[2,256,256]{2,1,0:T(8,128)}, f32[2,256,256]...) custom-call(f32[1,256,256]{2,1,0:T(8,128)S(1)} %get-tuple-element.14.refs_0_, ...), custom_call_target="tpu_custom_call" | custom-call | tf_op jit(solution)/shard_map/pallas_call | solution.py:1093

commit v7 on v6

--- a/solution.py
+++ b/solution.py
@@ -218,12 +218,13 @@
     core = lax.rem(me, 2)
     outer = lax.div(me, 2)
     mate = me + 1 - 2 * core
+    side = 2 * lax.div(2 * me, N) - 1
 
     barrier = pltpu.get_barrier_semaphore()
 
     def greet(step, carry):
         pl.semaphore_signal(
-            barrier, inc=1, device_id={"nodes": lax.rem(me + step, N)}, device_id_type=MESH
+            barrier, inc=1, device_id={"nodes": lax.rem(me + side * step + N, N)}, device_id_type=MESH
         )
         return carry
 
@@ -267,7 +268,7 @@
 
     def start_exchange(which, one_tile=False):
         def send(step, carry):
-            other = lax.rem(me + step, N)
+            other = lax.rem(me + side * step + N, N)
             place = 0 if one_tile else pl.multiple_of(other * TILE, TILE)
             pltpu.make_async_remote_copy(
                 src_ref=v.outgoing.at[which, pl.ds(place, TILE)],
@@ -826,7 +827,7 @@
         own = pl.ds(pl.multiple_of(me * TILE, TILE), TILE)
 
         def send(step, carry):
-            other = lax.rem(me + step, N)
+            other = lax.rem(me + side * step + N, N)
             pltpu.make_async_remote_copy(
                 src_ref=v.returning.at[pl.ds(pl.multiple_of(other * TILE, TILE), TILE)],
                 dst_ref=v.returned.at[own],

time: 57.6 us -> 57.1 us (level)
  no operation moved by 1% of the time
where the time goes in v7:
time: 57.1 us; the launch traced here: 56.9 us
  Pallas kernels  56.1 us (98%)
  between operations  0.81 us (1%)
    pallas_call x1, Pallas kernels, body(): pl.pallas_call(functools.partial(kernel, z, names), out_shape=tuple((pltp...  54.7 us
    pallas_call x1, Pallas kernels, body(): pl.pallas_call(store_kernel, out_shape=results, in_specs=[anywhere] * 6,...  1.41 us

profile of v7, /device:TPU:0, one launch (start us, length us, event | category | flops | bytes accessed | tf_op | source)
XLA Modules:
  0.0 56.9 jit_solution(4662647161998017650)
XLA Ops:
  0.6 54.7 %shard_map.179 = (f32[1,256,256]{2,1,0:T(8,128)S(1)}, f32[1,256,256]{2,1,0:T(8,128)S(1)}, f32[2,3,256,256]{3,2,1,0:T(8,128)S(1)}, f32[2,256]{1,0:T(2,128)S(1)}, ...) custom-call(f32[4,256,256]{2,1,0:T(8,128)} %refs_0_.1, f32[4,256,256]{2,1,0:T(8,128)} %refs_1_.1, s32[4,256]{1,0:T(4,128)} %refs_2_.1, ...), custom_call_target="tpu_custom_call" | custom-call | tf_op jit(solution)/shard_map/pallas_call | solution.py:1071
  55.4 1.4 %shard_map.180 = (f32[1,256,256]{2,1,0:T(8,128)}, f32[1,256,256]{2,1,0:T(8,128)}, f32[2,256,256]{2,1,0:T(8,128)}, f32[2,256,256]{2,1,0:T(8,128)}, f32[2,256,256]...) custom-call(f32[1,256,256]{2,1,0:T(8,128)S(1)} %get-tuple-element.14.refs_0_, ...), custom_call_target="tpu_custom_call" | custom-call | tf_op jit(solution)/shard_map/pallas_call | solution.py:1094

commit v8 on v7

--- a/solution.py
+++ b/solution.py
@@ -620,8 +620,8 @@
         def activate(slot):
             for place in range(0, R, BLOCK):
                 rows = pl.ds(place, BLOCK)
-                u = v.taken[layer, slot, rows, :] + v.right[layer, rows, :]
-                store_pair(slot, rows, u * sigmoid(u) * vector)
+                half = 0.5 * (v.taken[layer, slot, rows, :] + v.right[layer, rows, :])
+                store_pair(slot, rows, (half * jnp.tanh(half) + half) * vector)
 
         for slot in range(1, K + 3):
             if slot < K:
@@ -634,8 +634,9 @@
         def mix(i, carry):
             rows = chunk(i)
             count = jnp.broadcast_to(v.prep_t[rows, K : K + 1], (CHUNK, D))
-            scores = [
-                jnp.where(count > slot, v.score[slot, rows, :], MASKED_SCORE) for slot in range(K)
+            scores = [v.score[0, rows, :], v.score[1, rows, :]]
+            scores += [
+                jnp.where(count > slot, v.score[slot, rows, :], MASKED_SCORE) for slot in range(2, K)
             ]
             highest = functools.reduce(jnp.maximum, scores)
             powers = [jnp.exp(score - highest) for score in scores]

time: 57.1 us -> 57.1 us (level)
  no operation moved by 1% of the time
where the time goes in v8:
time: 57.1 us; the launch traced here: 57 us
  Pallas kernels  56.2 us (98%)
  between operations  0.81 us (1%)
    pallas_call x1, Pallas kernels, body(): pl.pallas_call(functools.partial(kernel, z, names), out_shape=tuple((pltp...  54.8 us
    pallas_call x1, Pallas kernels, body(): pl.pallas_call(store_kernel, out_shape=results, in_specs=[anywhere] * 6,...  1.41 us

profile of v8, /device:TPU:0, one launch (start us, length us, event | category | flops | bytes accessed | tf_op | source)
XLA Modules:
  0.0 57.0 jit_solution(5828761467674137316)
XLA Ops:
  0.6 54.8 %shard_map.179 = (f32[1,256,256]{2,1,0:T(8,128)S(1)}, f32[1,256,256]{2,1,0:T(8,128)S(1)}, f32[2,3,256,256]{3,2,1,0:T(8,128)S(1)}, f32[2,256]{1,0:T(2,128)S(1)}, ...) custom-call(f32[4,256,256]{2,1,0:T(8,128)} %refs_0_.1, f32[4,256,256]{2,1,0:T(8,128)} %refs_1_.1, s32[4,256]{1,0:T(4,128)} %refs_2_.1, ...), custom_call_target="tpu_custom_call" | custom-call | tf_op jit(solution)/shard_map/pallas_call | solution.py:1072
  55.4 1.4 %shard_map.180 = (f32[1,256,256]{2,1,0:T(8,128)}, f32[1,256,256]{2,1,0:T(8,128)}, f32[2,256,256]{2,1,0:T(8,128)}, f32[2,256,256]{2,1,0:T(8,128)}, f32[2,256,256]...) custom-call(f32[1,256,256]{2,1,0:T(8,128)S(1)} %get-tuple-element.14.refs_0_, ...), custom_call_target="tpu_custom_call" | custom-call | tf_op jit(solution)/shard_map/pallas_call | solution.py:1095
